TPU v7x, 256 devices: a whole 4x4x8 slice. The times are simulated.
256 devices in a mesh: mp: 4 (over z_lo), dp: 4 (over z_hi, core), tensor: 16 (over x, y).
Axes of the slice: x: 4, y: 4, z: 8 (z_hi: 2, z_lo: 4; z = z_hi * 4 + z_lo), core: 2. Of those that a mesh axis runs over, the one named last changes fastest.
Arguments:
- tokens: bfloat16 [1024, 8192], P(('mp', 'tensor'), 'dp'), may hold values from -64 to 64
- norm_gain: float32 [2, 8192], replicated, may hold values from 0.5 to 1.5
- gate_weight: bfloat16 [2, 8192, 14336], P(None, 'dp', ('mp', 'tensor')), may hold values from -0.0625 to 0.0625
- up_weight: bfloat16 [2, 8192, 14336], P(None, 'dp', ('mp', 'tensor')), may hold values from -0.0625 to 0.0625
- down_weight: bfloat16 [2, 14336, 8192], P(None, 'mp', 'tensor'), may hold values from -0.046875 to 0.046875
- sketch: bfloat16 [8192, 512], P('tensor'), may hold values from -6 to 6
Outputs:
- final_basis: float32 [8192, 512], P('tensor', ('mp', 'dp'))
- projected: float32 [8192, 512], P('tensor', ('mp', 'dp'))
All inputs are finite; a program needn't handle non-finite values.
Results may differ from a plain program's by a relative error of at most 0.04.
Values may be sent and summed in bfloat16 or wider, within the bound.
A program may use at most 128 MiB of HBM per device.

v0:
```python
import jax
import jax.numpy as jnp
from jax import lax
from jax.sharding import PartitionSpec as P

D = 8192


EPSILON = 1e-05
HIGHEST = lax.Precision.HIGHEST


def orthonormal_from(gram_total, matrix):
    lower_factor = jnp.linalg.cholesky(gram_total)
    return lax.linalg.triangular_solve(
        lower_factor, matrix, left_side=False, lower=True, transpose_a=True
    )


def gram_of(matrix):
    return lax.dot_general(matrix, matrix, (((0,), (0,)), ((), ())), precision=HIGHEST) / D


def orthonormal(partial_value):
    summed = lax.psum(partial_value, ("mp", "dp"))
    gram_total = lax.psum(gram_of(summed), "tensor")
    return orthonormal_from(gram_total, summed)


def sketch_product(left_acts, right_acts, matrix, tokens_all):
    inner_sums = lax.psum(jnp.dot(right_acts, matrix, precision=HIGHEST), "tensor")
    product = lax.dot_general(left_acts, inner_sums, (((0,), (0,)), ((), ())), precision=HIGHEST)
    return product / tokens_all


def project_block(block_normed, gate_weight, up_weight):
    gate_part = jnp.einsum(
        "crd,cdh->rch", block_normed, gate_weight, preferred_element_type=jnp.float32
    )
    up_part = jnp.einsum(
        "crd,cdh->rch", block_normed, up_weight, preferred_element_type=jnp.float32
    )
    return jnp.stack((gate_part, up_part), axis=2)


def on_device(tokens, norm_gain, gate_weight, up_weight, down_weight, sketch):
    token_groups = lax.axis_size(("mp", "tensor"))
    tokens_all = tokens.shape[0] * token_groups
    feature_count = tokens.shape[1]
    offset = lax.axis_index("dp") * feature_count
    local_gain = lax.dynamic_slice_in_dim(norm_gain, offset, feature_count, 1)
    gathered = lax.all_gather(tokens, ("mp", "tensor"), axis=0, tiled=True)
    values = gathered.astype(jnp.float32)
    square_total = lax.psum(jnp.sum(values * values, axis=1), "dp")
    inverse_root = lax.rsqrt(square_total / D + EPSILON)
    normed = (values[None, :, :] * inverse_root[None, :, None] * local_gain[:, None, :]).astype(
        jnp.bfloat16
    )
    summed = lax.psum_scatter(
        project_block(normed, gate_weight, up_weight).astype(jnp.bfloat16),
        "dp",
        scatter_dimension=0,
        tiled=True,
    ).astype(jnp.float32)
    hidden = (jax.nn.silu(summed[:, :, 0]) * summed[:, :, 1]).astype(jnp.bfloat16)
    partial_out = jnp.einsum(
        "rch,chd->rcd",
        lax.all_gather(hidden, "tensor", axis=2, tiled=True),
        down_weight,
        preferred_element_type=jnp.float32,
    )
    layer_out = lax.psum_scatter(partial_out, "mp", scatter_dimension=0, tiled=True)
    base_acts = layer_out[:, 0, :]
    inst_acts = layer_out[:, 1, :]
    first_basis = orthonormal(
        sketch_product(base_acts, inst_acts, sketch.astype(jnp.float32), tokens_all)
    )
    second_basis = orthonormal(sketch_product(inst_acts, base_acts, first_basis, tokens_all))
    final_basis = orthonormal(sketch_product(base_acts, inst_acts, second_basis, tokens_all))
    core_part = sketch_product(inst_acts, base_acts, final_basis, tokens_all)
    projected = lax.psum_scatter(core_part, ("mp", "dp"), scatter_dimension=1, tiled=True)
    share_width = final_basis.shape[1] // lax.axis_size(("mp", "dp"))
    basis_share = lax.dynamic_slice_in_dim(
        final_basis, lax.axis_index(("mp", "dp")) * share_width, share_width, 1
    )
    return (basis_share, projected)


def solution(mesh):
    return jax.shard_map(
        on_device,
        mesh=mesh,
        in_specs=(
            P(("mp", "tensor"), "dp"),
            P(),
            P(None, "dp", ("mp", "tensor")),
            P(None, "dp", ("mp", "tensor")),
            P(None, "mp", "tensor"),
            P("tensor", None),
        ),
        out_specs=(P("tensor", ("mp", "dp")), P("tensor", ("mp", "dp"))),
        check_vma=False,
    )
```

profile of v0, /device:TPU:1, one launch (start us, length us, event | category | flops | bytes accessed | tf_op | source)
XLA Modules:
  0.0 2116.3 jit_solution(5251044405594722481)
XLA Ops:
  8.7 316.9 %all-gather.3.cloned.1.call-done = bf16[1024,2048]{1,0:T(8,128)(2,1)} async-done(((bf16[16,2048]{1,0:T(8,128)(2,1)}), bf16[1024,2048]{1,0:T(8,128)(2,1)}) %all-gather.3.cloned.1.call-update) | async-done | bytes 4194320 | tf_op jit(solution)/shard_map/all_gather | solution.py:52
  328.7 50.9 %psum.77 = f32[1024]{0:T(1024)S(1)} all-reduce(f32[1024]{0:T(1024)S(1)} %fusion.2), channel_id=1, replica_groups=mesh['mp'=4,'dp'=4,'tensor'=16] {'dp'}, use_global_device_ids=true, to_apply=%region_1.0 | all-reduce | flops 1024 | bytes 8192 | tf_op jit(solution)/shard_map/psum | solution.py:54
  399.5 52.8 %reduce-scatter.6.cloned.1.call-done = bf16[256,2,2,224]{0,3,1,2:T(8,128)(2,1)} async-done(((bf16[1024,2,2,224]{0,3,1,2:T(8,128)(2,1)}), bf16[256,2,2,224]{0,3,1,2:T(8,128)(2,1)}) %reduce-scatter.6.cloned.1.call-update) | async-done | bytes 458768 | tf_op jit(solution)/shard_map/reduce_scatter | solution.py:59
  454.4 51.2 %all-gather.5.cloned.1.call-done = bf16[256,2,3584]{0,2,1:T(8,128)(2,1)} async-done(((bf16[256,2,224]{0,2,1:T(8,128)(2,1)}), bf16[256,2,3584]{0,2,1:T(8,128)(2,1)}) %all-gather.5.cloned.1.call-update) | async-done | bytes 3670032 | tf_op jit(solution)/shard_map/all_gather | solution.py:68
  512.9 32.0 %reduce-scatter.8.cloned.1.call-done = f32[64,2,512]{2,0,1:T(8,128)} async-done(((f32[256,2,512]{2,0,1:T(8,128)}), f32[64,2,512]{2,0,1:T(8,128)}) %reduce-scatter.8.cloned.1.call-update) | async-done | bytes 262160 | tf_op jit(solution)/shard_map/reduce_scatter | solution.py:72
  546.9 90.9 %all-reduce.12.cloned.1.call-done = f32[64,512]{1,0:T(8,128)} async-done(((f32[64,512]{1,0:T(8,128)}), f32[64,512]{1,0:T(8,128)}) %all-reduce.12.cloned.1.call-update) | async-done | bytes 131088 | tf_op jit(solution)/shard_map/psum | solution.py:31
  641.0 112.3 %all-reduce.14.cloned.1.call-done = f32[512,512]{1,0:T(8,128)} async-done(((f32[512,512]{1,0:T(8,128)}), f32[512,512]{1,0:T(8,128)}) %all-reduce.14.cloned.1.call-update) | async-done | bytes 1048592 | tf_op jit(solution)/shard_map/psum | solution.py:25
  758.0 96.0 %all-reduce.16.cloned.1.call-done = f32[512,512]{0,1:T(8,128)} async-done(((f32[512,512]{0,1:T(8,128)}), f32[512,512]{0,1:T(8,128)}) %all-reduce.16.cloned.1.call-update) | async-done | bytes 1048592 | tf_op jit(solution)/shard_map/psum | solution.py:26
  858.1 11.7 cholesky.374
  882.3 11.7 cholesky.393
  905.6 11.7 cholesky.414
  929.3 11.7 cholesky.431
  957.9 39.3 %custom-call.34 = f32[4,128,128]{1,2,0:T(8,128)S(1)} custom-call(f32[4,128,128]{2,1,0:T(8,128)S(1)} %get-tuple-element.24), custom_call_target="InvertDiagBlocksLowerTriangular" | custom-call | tf_op jit(solution)/shard_map/triangular_solve/custom-call.3 | solution.py:15
  1006.5 91.7 %all-reduce.18.cloned.1.call-done = f32[64,512]{1,0:T(8,128)} async-done(((f32[64,512]{1,0:T(8,128)}), f32[64,512]{1,0:T(8,128)}) %all-reduce.18.cloned.1.call-update) | async-done | bytes 131088 | tf_op jit(solution)/shard_map/psum | solution.py:31
  1101.2 112.3 %all-reduce.20.cloned.1.call-done = f32[512,512]{1,0:T(8,128)} async-done(((f32[512,512]{1,0:T(8,128)}), f32[512,512]{1,0:T(8,128)}) %all-reduce.20.cloned.1.call-update) | async-done | bytes 1048592 | tf_op jit(solution)/shard_map/psum | solution.py:25
  1218.2 96.0 %all-reduce.22.cloned.1.call-done = f32[512,512]{0,1:T(8,128)} async-done(((f32[512,512]{0,1:T(8,128)}), f32[512,512]{0,1:T(8,128)}) %all-reduce.22.cloned.1.call-update) | async-done | bytes 1048592 | tf_op jit(solution)/shard_map/psum | solution.py:26
  1318.3 11.7 cholesky.446
  1418.7 39.3 %custom-call.38 = f32[4,128,128]{1,2,0:T(8,128)S(1)} custom-call(f32[4,128,128]{2,1,0:T(8,128)S(1)} %get-tuple-element.25), custom_call_target="InvertDiagBlocksLowerTriangular" | custom-call | tf_op jit(solution)/shard_map/triangular_solve/custom-call.3 | solution.py:15
  1467.3 91.7 %all-reduce.24.cloned.1.call-done = f32[64,512]{1,0:T(8,128)} async-done(((f32[64,512]{1,0:T(8,128)}), f32[64,512]{1,0:T(8,128)}) %all-reduce.24.cloned.1.call-update) | async-done | bytes 131088 | tf_op jit(solution)/shard_map/psum | solution.py:31
  1562.0 112.3 %all-reduce.26.cloned.1.call-done = f32[512,512]{1,0:T(8,128)} async-done(((f32[512,512]{1,0:T(8,128)}), f32[512,512]{1,0:T(8,128)}) %all-reduce.26.cloned.1.call-update) | async-done | bytes 1048592 | tf_op jit(solution)/shard_map/psum | solution.py:25
  1679.0 96.0 %all-reduce.28.cloned.1.call-done = f32[512,512]{0,1:T(8,128)} async-done(((f32[512,512]{0,1:T(8,128)}), f32[512,512]{0,1:T(8,128)}) %all-reduce.28.cloned.1.call-update) | async-done | bytes 1048592 | tf_op jit(solution)/shard_map/psum | solution.py:26
  1879.4 39.3 %custom-call.42 = f32[4,128,128]{1,2,0:T(8,128)S(1)} custom-call(f32[4,128,128]{2,1,0:T(8,128)S(1)} %get-tuple-element.26), custom_call_target="InvertDiagBlocksLowerTriangular" | custom-call | tf_op jit(solution)/shard_map/triangular_solve/custom-call.3 | solution.py:15
  1932.5 91.7 %all-reduce.30.cloned.1.call-done = f32[64,512]{1,0:T(8,128)} async-done(((f32[64,512]{1,0:T(8,128)}), f32[64,512]{1,0:T(8,128)}) %all-reduce.30.cloned.1.call-update) | async-done | bytes 131088 | tf_op jit(solution)/shard_map/psum | solution.py:31
  2029.3 80.0 %reduce-scatter.10.cloned.1.call-done = f32[32,512]{1,0:T(8,128)} async-done(((f32[512,512]{1,0:T(8,128)}), f32[32,512]{1,0:T(8,128)}) %reduce-scatter.10.cloned.1.call-update) | async-done | bytes 65552
  (225 shorter events, 376.5 us)
Async XLA Ops:
  7.2 378.4 %copy-start = (bf16[2,2048,224]{1,2,0:T(8,128)(2,1)S(1)}, bf16[2,2048,224]{1,2,0:T(8,128)(2,1)}, u32[]{:S(2)}) copy-start(bf16[2,2048,224]{1,2,0:T(8,128)(2,1)} %param.11) | copy-start | bytes 5505028
  7.2 318.4 %all-gather.3.cloned.1.call-start = ((), (), s32[]{:S(2)}) async-start(), calls=%async_computation.3 | async-start | bytes 4259840 | tf_op jit(solution)/shard_map/all_gather | solution.py:52
  7.9 444.4 %reduce-scatter.6.cloned.1.call-start = ((), (), s32[]{:S(2)}) async-start(), calls=%async_computation.4 | async-start | bytes 2293760 | tf_op jit(solution)/shard_map/reduce_scatter | solution.py:59
  385.6 6.2 copy-start.13
  399.5 106.1 %all-gather.5.cloned.1.call-start = ((), (), s32[]{:S(2)}) async-start(), calls=%async_computation.5 | async-start | bytes 3899392 | tf_op jit(solution)/shard_map/all_gather | solution.py:68
  454.3 90.6 %copy-start.11 = (bf16[512,512]{1,0:T(8,128)(2,1)S(1)}, bf16[512,512]{1,0:T(8,128)(2,1)}, u32[]{:S(2)}) copy-start(bf16[512,512]{1,0:T(8,128)(2,1)} %param.14) | copy-start | bytes 1572868
  454.3 90.6 %reduce-scatter.8.cloned.1.call-start = ((), (), s32[]{:S(2)}) async-start(), calls=%async_computation.6 | async-start | bytes 1310720 | tf_op jit(solution)/shard_map/reduce_scatter | solution.py:72
  512.9 125.0 %all-reduce.12.cloned.1.call-start = ((), (), s32[]{:S(2)}) async-start(), calls=%async_computation.7 | async-start | bytes 262144 | tf_op jit(solution)/shard_map/psum | solution.py:31
  546.9 206.4 %all-reduce.14.cloned.1.call-start = ((), (), s32[]{:S(2)}) async-start(), calls=%async_computation.8 | async-start | bytes 2097152 | tf_op jit(solution)/shard_map/psum | solution.py:25
  640.9 213.1 %all-reduce.16.cloned.1.call-start = ((), (), s32[]{:S(2)}) async-start(), calls=%async_computation.9 | async-start | bytes 2097152 | tf_op jit(solution)/shard_map/psum | solution.py:26
  757.7 239.5 %copy-start.2 = (f32[512,512]{1,0:T(8,128)S(1)}, f32[512,512]{1,0:T(8,128)}, u32[]{:S(2)}) copy-start(f32[512,512]{1,0:T(8,128)} %all-reduce.14.cloned.1.call-done) | copy-start | bytes 3145732
  757.7 340.4 %all-reduce.18.cloned.1.call-start = ((), (), s32[]{:S(2)}) async-start(), calls=%async_computation.10 | async-start | bytes 262144 | tf_op jit(solution)/shard_map/psum | solution.py:31
  858.0 146.6 %copy-start.9 = (f32[64,2,512]{2,0,1:T(8,128)S(1)}, f32[64,2,512]{2,0,1:T(8,128)}, u32[]{:S(2)}) copy-start(f32[64,2,512]{2,0,1:T(8,128)} %reduce-scatter.8.cloned.1.call-done) | copy-start | bytes 786436
  1006.5 207.1 %all-reduce.20.cloned.1.call-start = ((), (), s32[]{:S(2)}) async-start(), calls=%async_computation.11 | async-start | bytes 2097152 | tf_op jit(solution)/shard_map/psum | solution.py:25
  1101.2 213.0 %all-reduce.22.cloned.1.call-start = ((), (), s32[]{:S(2)}) async-start(), calls=%async_computation.12 | async-start | bytes 2097152 | tf_op jit(solution)/shard_map/psum | solution.py:26
  1217.9 240.1 %copy-start.4 = (f32[512,512]{1,0:T(8,128)S(1)}, f32[512,512]{1,0:T(8,128)}, u32[]{:S(2)}) copy-start(f32[512,512]{1,0:T(8,128)} %all-reduce.20.cloned.1.call-done) | copy-start | bytes 3145732
  1218.0 341.0 %all-reduce.24.cloned.1.call-start = ((), (), s32[]{:S(2)}) async-start(), calls=%async_computation.13 | async-start | bytes 262144 | tf_op jit(solution)/shard_map/psum | solution.py:31
  1467.2 207.1 %all-reduce.26.cloned.1.call-start = ((), (), s32[]{:S(2)}) async-start(), calls=%async_computation.14 | async-start | bytes 2097152 | tf_op jit(solution)/shard_map/psum | solution.py:25
  1562.0 213.1 %all-reduce.28.cloned.1.call-start = ((), (), s32[]{:S(2)}) async-start(), calls=%async_computation.15 | async-start | bytes 2097152 | tf_op jit(solution)/shard_map/psum | solution.py:26
  1678.7 240.0 %copy-start.3 = (f32[512,512]{1,0:T(8,128)S(1)}, f32[512,512]{1,0:T(8,128)}, u32[]{:S(2)}) copy-start(f32[512,512]{1,0:T(8,128)} %all-reduce.26.cloned.1.call-done) | copy-start | bytes 3145732
  1678.8 345.4 %all-reduce.30.cloned.1.call-start = ((), (), s32[]{:S(2)}) async-start(), calls=%async_computation.16 | async-start | bytes 262144 | tf_op jit(solution)/shard_map/psum | solution.py:31
  1879.3 229.9 %copy-start.1 = (bf16[2,2048,224]{1,2,0:T(8,128)(2,1)S(1)}, bf16[2,2048,224]{1,2,0:T(8,128)(2,1)}, u32[]{:S(2)}) copy-start(bf16[2,2048,224]{1,2,0:T(8,128)(2,1)} %param.11) | copy-start | bytes 5505028
  1925.3 3.8 copy-start.8
  1932.4 176.8 %reduce-scatter.10.cloned.1.call-start = ((), (), s32[]{:S(2)}) async-start(), calls=%async_computation.17 | async-start | bytes 1114112
  (5 other events, 4.5 us)
Sparse Core Ops, SparseCore 0:
  9.8 315.7 all-gather.2
  399.6 52.7 reduce-scatter.5
  455.1 50.4 all-gather.4
  513.0 31.8 reduce-scatter.7
  548.0 89.8 all-reduce.11
  641.1 112.1 all-reduce.13
  757.8 96.1 all-reduce.15
  1006.6 91.5 all-reduce.17
  1101.3 112.1 all-reduce.19
  1218.1 96.0 all-reduce.21
  1467.4 91.5 all-reduce.23
  1562.1 112.1 all-reduce.25
  1678.9 96.1 all-reduce.27
  1932.6 91.5 all-reduce.29
  2027.6 81.5 reduce-scatter.9
where the time goes:
time: 2130 us; the launch traced here: 2120 us
  waiting for transfers between devices  1520 us (71%)
  other arithmetic  377 us (18%)
  matrix products  93.2 us (4%)
  blocking collectives  50.9 us (2%)
  local copies, waits for them, and re-layouts  46.1 us (2%)
  between operations  22.6 us (1%)
    psum x4, waiting for transfers between devices, sketch_product(): lax.psum(jnp.dot(right_acts, matrix, precision=HIGHEST), 'tensor')  366 us
    psum x3, waiting for transfers between devices, orthonormal(): summed = lax.psum(partial_value, ('mp', 'dp'))  337 us
    all_gather x1, waiting for transfers between devices, on_device(): gathered = lax.all_gather(tokens, ('mp', 'tensor'), axis=0, tiled=True)  317 us
    psum x3, waiting for transfers between devices, orthonormal(): gram_total = lax.psum(gram_of(summed), 'tensor')  288 us
    another operation x44, other arithmetic, orthonormal_from(): lower_factor = jnp.linalg.cholesky(gram_total)  237 us
    another operation x8, other arithmetic, orthonormal_from(): lax.linalg.triangular_solve(lower_factor, matrix, left_side=False, lower=...  124 us
    unnamed x16, waiting for transfers between devices  80.9 us
    reduce_scatter x1, waiting for transfers between devices, on_device(): lax.psum_scatter(project_block(normed, gate_weight, up_weight).astype(jnp...  52.8 us
  transfers between devices with their start and end apart: 15, of which 15 were waited for; matrix products, arithmetic and copies ran while one was open for 0% of the time, Pallas kernels for 0%

commit v1 on v0

v1 whole, which is shorter than its diff:
```python
import functools

import jax
import jax.numpy as jnp
from jax import lax
from jax.experimental import pallas as pl
from jax.experimental.pallas import tpu as pltpu
from jax.sharding import PartitionSpec as P

D = 8192
EPSILON = 1e-05
BLOCK = 128


def split(value):
    high = value.astype(jnp.bfloat16)
    return high, (value - high.astype(jnp.float32)).astype(jnp.bfloat16)


def mul(left, right, contract=((1,), (0,))):
    def dot(a, b):
        return lax.dot_general(a, b, (contract, ((), ())), preferred_element_type=jnp.float32)

    (a, a_low), (b, b_low) = left, right
    return dot(a, b) + (dot(a, b_low) + dot(a_low, b))


def inverse_factor(rows):
    lane = lax.broadcasted_iota(jnp.int32, (8, BLOCK), 1)
    sub = lax.broadcasted_iota(jnp.int32, (8, BLOCK), 0)
    rows = list(rows)
    for j in range(BLOCK):
        g, s = divmod(j, 8)
        at_j = lane == j
        below = sub > s
        row = rows[g][s : s + 1, :]
        inv = 1.0 / row[:, j : j + 1]
        scaled = jnp.where(at_j, 1.0, jnp.broadcast_to(row, (8, BLOCK))) * inv
        for h in range(g, BLOCK // 8):
            old = rows[h]
            col = jnp.broadcast_to(old[:, j : j + 1], (8, BLOCK))
            if h == g:
                new = jnp.where(at_j, 0.0, old) - col * scaled
                rows[h] = jnp.where(below, new, old)
            else:
                rows[h] = jnp.where(at_j, 0.0, old) - col * scaled
    out = []
    for g in range(BLOCK // 8):
        row_index = sub + 8 * g
        pivot = jnp.sum(jnp.where(lane == row_index, rows[g], 0.0), axis=1, keepdims=True)
        unit = jnp.where(lane == row_index, 1.0, jnp.where(lane < row_index, rows[g], 0.0))
        out.append(unit * lax.rsqrt(pivot))
    return jnp.concatenate(out, axis=0)


def orth_factor(gram, low_inv):
    n = gram.shape[0] // BLOCK
    low_inv[...] = jnp.zeros_like(low_inv)

    def step(k, carry):
        base = pl.multiple_of(k * BLOCK, BLOCK)
        here = pl.ds(base, BLOCK)
        rows = [gram[pl.ds(pl.multiple_of(base + 8 * g, 8), 8), here] for g in range(BLOCK // 8)]
        inv = inverse_factor(rows)
        inv_s = split(inv)
        panel = mul(inv_s, split(gram[here, :]))
        lane = lax.broadcasted_iota(jnp.int32, panel.shape, 1)
        panel = jnp.where(lane >= base + BLOCK, panel, 0.0)
        low_inv[here, here] = inv
        done = mul(inv_s, split(low_inv[here, :] * jnp.where(lane < base, 1.0, 0.0)))
        mine = jnp.where(lane < base, done, low_inv[here, :])
        low_inv[here, :] = mine
        panel_s = split(panel)
        gram[...] -= mul(panel_s, panel_s, ((0,), (0,)))
        low_inv[...] -= mul(panel_s, split(mine), ((0,), (0,)))
        return carry

    lax.fori_loop(0, n, step, 0)


def sketch_kernel(g0_ref, g1_ref, z_ref, out_ref, low_ref, gram, low_inv, high_z, low_z):
    tokens, rank = z_ref.shape

    def rank_step(which, g_ref):
        g_s = split(g_ref[...])
        z_s = split(z_ref[...]) if which == 0 else (high_z[...], low_z[...])
        h = mul(g_s, z_s)
        gram[...] = mul(z_s, split(h), ((0,), (0,))) * (2.0**-33)
        orth_factor(gram, low_inv)
        return h, z_s

    def advance(h):
        z = mul(split(h * (1.0 / 1024)), split(low_inv[...]), ((1,), (1,)))
        high, low = split(z)
        high_z[...] = high
        low_z[...] = low

    h, _ = rank_step(0, g0_ref)
    advance(h)
    h, _ = rank_step(1, g1_ref)
    advance(h)
    _, z_s = rank_step(2, g0_ref)
    basis = mul(z_s, split(low_inv[...]), ((1,), (1,))) * (1.0 / 1024)
    high, low = split(basis)
    out_ref[...] = high
    low_ref[...] = low


def sketch_call(gram0, gram1, z):
    tokens, rank = z.shape
    return pl.pallas_call(
        sketch_kernel,
        out_shape=(jax.ShapeDtypeStruct((tokens, rank), jnp.bfloat16),) * 2,
        in_specs=[pl.BlockSpec(memory_space=pltpu.VMEM)] * 3,
        out_specs=(pl.BlockSpec(memory_space=pltpu.VMEM),) * 2,
        scratch_shapes=[
            pltpu.VMEM((rank, rank), jnp.float32),
            pltpu.VMEM((rank, rank), jnp.float32),
            pltpu.VMEM((tokens, rank), jnp.bfloat16),
            pltpu.VMEM((tokens, rank), jnp.bfloat16),
        ],
        compiler_params=pltpu.CompilerParams(vmem_limit_bytes=56 * 2**20),
    )(gram0, gram1, z)


def project_block(block_normed, gate_weight, up_weight):
    gate_part = jnp.einsum(
        "crd,cdh->rch", block_normed, gate_weight, preferred_element_type=jnp.float32
    )
    up_part = jnp.einsum(
        "crd,cdh->rch", block_normed, up_weight, preferred_element_type=jnp.float32
    )
    return jnp.stack((gate_part, up_part), axis=2)


def on_device(tokens, norm_gain, gate_weight, up_weight, down_weight, sketch):
    feature_count = tokens.shape[1]
    offset = lax.axis_index("dp") * feature_count
    local_gain = lax.dynamic_slice_in_dim(norm_gain, offset, feature_count, 1)
    gathered = lax.all_gather(tokens, ("mp", "tensor"), axis=0, tiled=True)
    values = gathered.astype(jnp.float32)
    square_total = lax.psum(jnp.sum(values * values, axis=1), "dp")
    inverse_root = lax.rsqrt(square_total / D + EPSILON)
    normed = (values[None, :, :] * inverse_root[None, :, None] * local_gain[:, None, :]).astype(
        jnp.bfloat16
    )
    summed = lax.psum_scatter(
        project_block(normed, gate_weight, up_weight).astype(jnp.bfloat16),
        "dp",
        scatter_dimension=0,
        tiled=True,
    ).astype(jnp.float32)
    hidden = (jax.nn.silu(summed[:, :, 0]) * summed[:, :, 1]).astype(jnp.bfloat16)
    partial_out = jnp.einsum(
        "rch,chd->crd",
        lax.all_gather(hidden, "tensor", axis=2, tiled=True),
        down_weight,
        preferred_element_type=jnp.float32,
    )
    layer_out = lax.psum_scatter(partial_out, "mp", scatter_dimension=1, tiled=True)
    mine = layer_out.astype(jnp.bfloat16)
    acts = lax.all_gather(mine, ("dp", "mp"), axis=1, tiled=True)

    def against(left, right, dims):
        return lax.dot_general(left, right, (dims, ((), ())), preferred_element_type=jnp.float32)

    rows = jnp.concatenate(
        [
            against(mine[0], acts[0], ((1,), (1,))),
            against(mine[1], acts[1], ((1,), (1,))),
            against(mine[1], sketch, ((1,), (0,))),
        ],
        axis=1,
    )
    rows = lax.psum(rows, "tensor")
    full = lax.all_gather(rows, ("dp", "mp"), axis=0, tiled=True)
    count = acts.shape[1]
    gram0, gram1, z = full[:, :count], full[:, count : 2 * count], full[:, 2 * count :]
    high, low = sketch_call(gram0, gram1, z)
    share = high.shape[1] // lax.axis_size(("mp", "dp"))
    start = lax.axis_index(("mp", "dp")) * share
    high = lax.dynamic_slice_in_dim(high, start, share, 1)
    low = lax.dynamic_slice_in_dim(low, start, share, 1)
    last = mul(split(gram0), (high, low)) * (1.0 / count)
    basis_share = against(acts[0], high, ((0,), (0,))) + against(acts[0], low, ((0,), (0,)))
    last_high, last_low = split(last)
    projected = against(acts[1], last_high, ((0,), (0,))) + against(
        acts[1], last_low, ((0,), (0,))
    )
    return (basis_share, projected)


def solution(mesh):
    return jax.shard_map(
        on_device,
        mesh=mesh,
        in_specs=(
            P(("mp", "tensor"), "dp"),
            P(),
            P(None, "dp", ("mp", "tensor")),
            P(None, "dp", ("mp", "tensor")),
            P(None, "mp", "tensor"),
            P("tensor", None),
        ),
        out_specs=(P("tensor", ("mp", "dp")), P("tensor", ("mp", "dp"))),
        check_vma=False,
    )
```

time: 2130 us -> 1170 us (0.55)
  waiting for transfers between devices: 1520 us -> 788 us
  other arithmetic: 377 us -> 15 us
  Pallas kernels: 0 us -> 246 us
  matrix products: 93.2 us -> 36.9 us
  local copies, waits for them, and re-layouts: 46.1 us -> 12.3 us
    psum x10 -> x1, waiting for transfers between devices: 991 us -> 93.7 us  [on_device(): rows = lax.psum(rows, 'tensor')]
    another operation x52 -> x0, other arithmetic: 361 us -> none  [the longest x44 237 us: orthonormal_from(): lower_factor = jnp.linalg.cholesky(gram_total)]
    pallas_call x0 -> x1, Pallas kernels: none -> 246 us  [sketch_call(): pl.pallas_call(sketch_kernel, out_shape=(jax.ShapeDtypeStruct((tokens, ra...]
    all_gather x0 -> x2, waiting for transfers between devices: none -> 240 us  [the longest x1 176 us: on_device(): full = lax.all_gather(rows, ('dp', 'mp'), axis=0, tiled=True)]
    unnamed x16 -> x7, waiting for transfers between devices: 80.9 us -> 0.78 us
    another operation x39 -> x0, matrix products: 41.2 us -> none  [the longest x21 24.8 us: orthonormal_from(): lax.linalg.triangular_solve(lower_factor, matrix, left_side=False, lower=...]
    another operation x52 -> x0, local copies, waits for them, and re-layouts: 34.6 us -> none  [the longest x40 34.2 us: orthonormal_from(): lax.linalg.triangular_solve(lower_factor, matrix, left_side=False, lower=...]
  transfers between devices with their start and end apart: 15 -> 7, of which waited for: 15 -> 7; matrix products, arithmetic and copies ran while one was open for 0% -> 0% of each run, Pallas kernels for 0% -> 0%
where the time goes in v1:
time: 1170 us; the launch traced here: 1160 us
  waiting for transfers between devices  788 us (67%)
  Pallas kernels  246 us (21%)
  blocking collectives  50.9 us (4%)
  matrix products  36.9 us (3%)
  other arithmetic  15 us (1%)
  between operations  14.5 us (1%)
  local copies, waits for them, and re-layouts  12.3 us (1%)
    all_gather x1, waiting for transfers between devices, on_device(): gathered = lax.all_gather(tokens, ('mp', 'tensor'), axis=0, tiled=True)  317 us
    pallas_call x1, Pallas kernels, sketch_call(): pl.pallas_call(sketch_kernel, out_shape=(jax.ShapeDtypeStruct((tokens, ra...  246 us
    all_gather x1, waiting for transfers between devices, on_device(): full = lax.all_gather(rows, ('dp', 'mp'), axis=0, tiled=True)  176 us
    psum x1, waiting for transfers between devices, on_device(): rows = lax.psum(rows, 'tensor')  93.7 us
    all_gather x1, waiting for transfers between devices, on_device(): acts = lax.all_gather(mine, ('dp', 'mp'), axis=1, tiled=True)  64.5 us
    reduce_scatter x1, waiting for transfers between devices, on_device(): lax.psum_scatter(project_block(normed, gate_weight, up_weight).astype(jnp...  52.8 us
    all_gather x1, waiting for transfers between devices, on_device(): lax.all_gather(hidden, 'tensor', axis=2, tiled=True)  51.2 us
    psum x1, blocking collectives, on_device(): square_total = lax.psum(jnp.sum(values * values, axis=1), 'dp')  50.9 us
  transfers between devices with their start and end apart: 7, of which 7 were waited for; matrix products, arithmetic and copies ran while one was open for 0% of the time, Pallas kernels for 0%

profile of v1, /device:TPU:1, one launch (start us, length us, event | category | flops | bytes accessed | tf_op | source)
XLA Modules:
  0.0 1164.2 jit_solution(6563273601772514235)
XLA Ops:
  8.7 316.9 %all-gather.5.cloned.1.call-done = bf16[1024,2048]{1,0:T(8,128)(2,1)} async-done(((bf16[16,2048]{1,0:T(8,128)(2,1)}), bf16[1024,2048]{1,0:T(8,128)(2,1)}) %all-gather.5.cloned.1.call-update) | async-done | bytes 4194320 | tf_op jit(solution)/shard_map/all_gather | solution.py:140
  325.6 3.1 fusion.2
  328.7 50.9 %psum.14 = f32[1024]{0:T(1024)S(1)} all-reduce(f32[1024]{0:T(1024)S(1)} %fusion.2), channel_id=1, replica_groups=mesh['mp'=4,'dp'=4,'tensor'=16] {'dp'}, use_global_device_ids=true, to_apply=%region_1.0 | all-reduce | flops 1024 | bytes 8192 | tf_op jit(solution)/shard_map/psum | solution.py:142
  379.6 6.0 convert_multiply_fusion
  385.6 6.2 fusion.10
  391.8 6.2 fusion.11
  398.0 1.4 pad_maximum_fusion
  399.5 52.8 %reduce-scatter.3.cloned.1.call-done = bf16[256,2,2,224]{0,3,1,2:T(8,128)(2,1)} async-done(((bf16[1024,2,2,224]{0,3,1,2:T(8,128)(2,1)}), bf16[256,2,2,224]{0,3,1,2:T(8,128)(2,1)}) %reduce-scatter.3.cloned.1.call-update) | async-done | bytes 458768 | tf_op jit(solution)/shard_map/reduce_scatter | solution.py:147
  454.4 51.2 %all-gather.7.cloned.1.call-done = bf16[256,2,3584]{0,2,1:T(8,128)(2,1)} async-done(((bf16[256,2,224]{0,2,1:T(8,128)(2,1)}), bf16[256,2,3584]{0,2,1:T(8,128)(2,1)}) %all-gather.7.cloned.1.call-update) | async-done | bytes 3670032 | tf_op jit(solution)/shard_map/all_gather | solution.py:156
  505.6 7.3 fusion.43
  513.0 32.0 %reduce-scatter.5.cloned.1.call-done = f32[2,64,512]{2,1,0:T(8,128)} async-done(((f32[2,256,512]{2,1,0:T(8,128)}), f32[2,64,512]{2,1,0:T(8,128)}) %reduce-scatter.5.cloned.1.call-update) | async-done | bytes 262160 | tf_op jit(solution)/shard_map/reduce_scatter | solution.py:160
  545.0 1.6 convert_element_type.38
  547.7 64.5 %all-gather.9.cloned.1.call-done = bf16[2,1024,512]{2,1,0:T(8,128)(2,1)} async-done(((bf16[2,64,512]{2,1,0:T(8,128)(2,1)}), bf16[2,1024,512]{2,1,0:T(8,128)(2,1)}) %all-gather.9.cloned.1.call-update) | async-done | bytes 2097168 | tf_op jit(solution)/shard_map/all_gather | solution.py:162
  612.2 1.7 fusion.18
  613.9 1.7 fusion.16
  617.0 93.7 %all-reduce.2.cloned.1.call-done = f32[64,2560]{1,0:T(8,128)} async-done(((f32[64,2560]{1,0:T(8,128)}), f32[64,2560]{1,0:T(8,128)}) %all-reduce.2.cloned.1.call-update) | async-done | bytes 655376 | tf_op jit(solution)/shard_map/psum | solution.py:175
  710.7 175.7 %all-gather.11.cloned.1.call-done = f32[1024,2560]{1,0:T(8,128)} async-done(((f32[64,2560]{1,0:T(8,128)}), f32[1024,2560]{1,0:T(8,128)}) %all-gather.11.cloned.1.call-update) | async-done | bytes 10485776 | tf_op jit(solution)/shard_map/all_gather | solution.py:176
  886.4 3.1 slice.49.z_ref
  889.5 8.5 fusion.42
  897.9 246.3 %shard_map.77 = (bf16[1024,512]{1,0:T(8,128)(2,1)}, bf16[1024,512]{1,0:T(8,128)(2,1)}) custom-call(f32[1024,1024]{1,0:T(8,128)} %get-tuple-element.7.g0_ref, f32[1024,1024]{1,0:T(8,128)} %get-tuple-element.6.g1_ref, f32[1024,512]{1,0:T(8,128)} %slice.49.z_ref), custom_call_target="tpu_custom_call" | custom-call | tf_op jit(solution)/shard_map/pallas_call | solution.py:111
  1144.2 1.5 fusion.15
  1145.7 3.0 fusion.25
  1148.8 3.0 fusion.21
  1152.9 3.0 fusion.14
  (33 shorter events, 8.5 us)
Async XLA Ops:
  7.2 378.4 %copy-start = (bf16[2,2048,224]{1,2,0:T(8,128)(2,1)S(1)}, bf16[2,2048,224]{1,2,0:T(8,128)(2,1)}, u32[]{:S(2)}) copy-start(bf16[2,2048,224]{1,2,0:T(8,128)(2,1)} %param.9) | copy-start | bytes 5505028
  7.2 318.4 %all-gather.5.cloned.1.call-start = ((), (), s32[]{:S(2)}) async-start(), calls=%async_computation.2 | async-start | bytes 4259840 | tf_op jit(solution)/shard_map/all_gather | solution.py:140
  7.9 444.4 %reduce-scatter.3.cloned.1.call-start = ((), (), s32[]{:S(2)}) async-start(), calls=%async_computation.3 | async-start | bytes 2293760 | tf_op jit(solution)/shard_map/reduce_scatter | solution.py:147
  385.6 6.2 copy-start.4
  399.5 106.1 %all-gather.7.cloned.1.call-start = ((), (), s32[]{:S(2)}) async-start(), calls=%async_computation.4 | async-start | bytes 3899392 | tf_op jit(solution)/shard_map/all_gather | solution.py:156
  454.3 92.3 %copy-start.2 = (bf16[512,512]{1,0:T(8,128)(2,1)S(1)}, bf16[512,512]{1,0:T(8,128)(2,1)}, u32[]{:S(2)}) copy-start(bf16[512,512]{1,0:T(8,128)(2,1)} %param.11) | copy-start | bytes 1572868
  454.3 90.6 %reduce-scatter.5.cloned.1.call-start = ((), (), s32[]{:S(2)}) async-start(), calls=%async_computation.5 | async-start | bytes 1310720 | tf_op jit(solution)/shard_map/reduce_scatter | solution.py:160
  512.9 99.3 %all-gather.9.cloned.1.call-start = ((), (), s32[]{:S(2)}) async-start(), calls=%async_computation.6 | async-start | bytes 2228224 | tf_op jit(solution)/shard_map/all_gather | solution.py:162
  546.6 164.1 %all-reduce.2.cloned.1.call-start = ((), (), s32[]{:S(2)}) async-start(), calls=%async_computation.7 | async-start | bytes 1310720 | tf_op jit(solution)/shard_map/psum | solution.py:175
  616.5 269.9 %all-gather.11.cloned.1.call-start = ((), (), s32[]{:S(2)}) async-start(), calls=%async_computation.8 | async-start | bytes 11141120 | tf_op jit(solution)/shard_map/all_gather | solution.py:176
  897.9 246.3 %copy-start.1 = (bf16[2,1024,512]{2,1,0:T(8,128)(2,1)S(1)}, bf16[2,1024,512]{2,1,0:T(8,128)(2,1)}, u32[]{:S(2)}) copy-start(bf16[2,1024,512]{2,1,0:T(8,128)(2,1)} %all-gather.9.cloned.1.call-done) | copy-start | bytes 6291460
  1144.2 4.5 copy-start.3
Sparse Core Ops, SparseCore 0:
  9.8 315.7 all-gather.4
  399.6 52.7 reduce-scatter.2
  455.1 50.4 all-gather.6
  513.0 31.8 reduce-scatter.4
  546.7 65.4 all-gather.8
  616.6 94.0 all-reduce.1
  712.5 173.8 all-gather.10

commit v2 on v1

--- a/solution.py
+++ b/solution.py
@@ -123,47 +123,469 @@
     )(gram0, gram1, z)
 
 
-def project_block(block_normed, gate_weight, up_weight):
-    gate_part = jnp.einsum(
-        "crd,cdh->rch", block_normed, gate_weight, preferred_element_type=jnp.float32
+MESH = pl.DeviceIdType.MESH
+VMEM = pl.BlockSpec(memory_space=pltpu.VMEM)
+
+
+class Sender:
+    def __init__(self, send, recv):
+        self.send, self.recv, self.all = send, recv, []
+
+    def __call__(self, source, target, device):
+        n = len(self.all)
+        copy = pltpu.make_async_remote_copy(
+            src_ref=source,
+            dst_ref=target,
+            send_sem=self.send.at[n],
+            recv_sem=self.recv.at[n],
+            device_id=device,
+            device_id_type=MESH,
+        )
+        copy.start()
+        self.all.append(copy)
+        return copy
+
+    def finish(self):
+        for copy in self.all:
+            copy.wait_send()
+
+
+def greet(peers):
+    barrier = pltpu.get_barrier_semaphore()
+    for peer in peers:
+        pl.semaphore_signal(barrier, inc=1, device_id=peer, device_id_type=MESH)
+    pl.semaphore_wait(barrier, len(peers))
+
+
+def grid_place():
+    t = lax.axis_index("tensor")
+    return t // 4, t % 4
+
+
+def ring(send, block, upper, lower, me, toward):
+    right, left = (me + 1) % 4, (me + 3) % 4
+    from_left = send(block(me), block(me), toward(right))
+    from_right = send(block(me), block(me), toward(left))
+
+    def forward():
+        from_left.wait_recv()
+        first = send(upper(left), upper(left), toward(right))
+        from_right.wait_recv()
+        second = send(lower(right), lower(right), toward(left))
+        return first, second
+
+    return forward
+
+
+def two_rings(send, piece_a, piece_b):
+    for phase in range(2):
+        a = ring(send, *piece_a(phase))
+        b = ring(send, *piece_b(phase))
+        pending = [*a(), *b()]
+        for copy in pending:
+            copy.wait_recv()
+
+
+def along_x(y):
+    return lambda i: {"tensor": i * 4 + y}
+
+
+def along_y(x):
+    return lambda i: {"tensor": x * 4 + i}
+
+
+def xy_neighbours(x, y):
+    return [
+        {"tensor": ((x + 1) % 4) * 4 + y},
+        {"tensor": ((x + 3) % 4) * 4 + y},
+        {"tensor": x * 4 + (y + 1) % 4},
+        {"tensor": x * 4 + (y + 3) % 4},
+    ]
+
+
+def tokens_kernel(x_ref, out, send_sem, recv_sem):
+    x, y = grid_place()
+    m = lax.axis_index("mp")
+    mates = [{"mp": (m + d) % 4} for d in range(1, 4)]
+    greet(mates + xy_neighbours(x, y))
+    send = Sender(send_sem, recv_sem)
+    rows = x_ref.shape[0]
+    half = x_ref.shape[1] // 2
+    mine = pl.ds(pl.multiple_of(m * rows, rows), rows)
+    first = [send(x_ref, out.at[x, y, mine], mate) for mate in mates]
+    out[x, y, mine] = x_ref[...]
+    for copy in first:
+        copy.wait_recv()
+    count = 4 * rows
+    a, b = pl.ds(0, half), pl.ds(half, half)
+    up, down = pl.ds(0, count // 2), pl.ds(count // 2, count // 2)
+    two, rest = pl.ds(0, 2), pl.ds(2, 2)
+
+    def piece_a(phase):
+        if phase == 0:
+            return (
+                lambda i: out.at[i, y, :, a],
+                lambda i: out.at[i, y, up, a],
+                lambda i: out.at[i, y, down, a],
+                x,
+                along_x(y),
+            )
+        return (
+            lambda i: out.at[:, i, :, a],
+            lambda i: out.at[two, i, :, a],
+            lambda i: out.at[rest, i, :, a],
+            y,
+            along_y(x),
+        )
+
+    def piece_b(phase):
+        if phase == 0:
+            return (
+                lambda i: out.at[x, i, :, b],
+                lambda i: out.at[x, i, up, b],
+                lambda i: out.at[x, i, down, b],
+                y,
+                along_y(x),
+            )
+        return (
+            lambda i: out.at[i, :, :, b],
+            lambda i: out.at[i, two, :, b],
+            lambda i: out.at[i, rest, :, b],
+            x,
+            along_x(y),
+        )
+
+    two_rings(send, piece_a, piece_b)
+    send.finish()
+
+
+def remote_call(kernel, out_shape, copies, number, scratch=(), limit=48):
+    return pl.pallas_call(
+        kernel,
+        out_shape=out_shape,
+        out_specs=VMEM,
+        scratch_shapes=[
+            *scratch,
+            pltpu.SemaphoreType.DMA((copies,)),
+            pltpu.SemaphoreType.DMA((copies,)),
+        ],
+        compiler_params=pltpu.CompilerParams(
+            collective_id=number, has_side_effects=True, vmem_limit_bytes=limit * 2**20
+        ),
     )
-    up_part = jnp.einsum(
-        "crd,cdh->rch", block_normed, up_weight, preferred_element_type=jnp.float32
-    )
-    return jnp.stack((gate_part, up_part), axis=2)
+
+
+def gather_tokens(tokens):
+    rows, features = tokens.shape
+    out = jax.ShapeDtypeStruct((4, 4, 4 * rows, features), tokens.dtype)
+    return remote_call(tokens_kernel, out, 19, 0)(tokens)
+
+
+def hidden_kernel(part, squares, out, near, near_sq, pair, pair_sq, far, far_sq, send_sem, recv_sem):
+    x, y = grid_place()
+    d = lax.axis_index("dp")
+    z, core = d // 2, d % 2
+    sibling, partner = {"dp": z * 2 + 1 - core}, {"dp": (1 - z) * 2 + core}
+    greet([sibling, partner] + xy_neighbours(x, y))
+    send = Sender(send_sem, recv_sem)
+    other, mine = (1 - z) * 2, z * 2
+    there = 1 - core
+    first = send(part.at[other + there], near.at[1], sibling)
+    first_sq = send(squares.at[other + there], near_sq.at[1], sibling)
+    second = send(part.at[mine + there], near.at[0], sibling)
+    second_sq = send(squares.at[mine + there], near_sq.at[0], sibling)
+    units = out.shape[3]
+    step = 32
+
+    first_sq.wait_recv()
+    pair_sq[...] = squares[other + core] + near_sq[1]
+    across_sq = send(pair_sq, far_sq, partner)
+    first.wait_recv()
+    across = []
+    for c in range(2):
+
+        @pl.loop(0, 2 * units // step)
+        def _(i):
+            rows = pl.ds(pl.multiple_of(c * 2 * units + i * step, step), step)
+            total = part[other + core, rows, :].astype(jnp.float32) + near[1, rows, :].astype(
+                jnp.float32
+            )
+            pair[rows, :] = total.astype(jnp.bfloat16)
+
+        rows = pl.ds(c * 2 * units, 2 * units)
+        across.append(send(pair.at[rows], far.at[rows], partner))
+
+    second_sq.wait_recv()
+    across_sq.wait_recv()
+    square_total = squares[mine + core] + near_sq[0] + far_sq[...]
+    root = lax.rsqrt(square_total[0:1, :] / D + EPSILON)
+    second.wait_recv()
+    for c in range(2):
+        across[c].wait_recv()
+
+        @pl.loop(0, units // step)
+        def _(i):
+            def total(row):
+                rows = pl.ds(pl.multiple_of(row + i * step, step), step)
+                return (
+                    part[mine + core, rows, :].astype(jnp.float32)
+                    + near[0, rows, :].astype(jnp.float32)
+                    + far[rows, :].astype(jnp.float32)
+                ) * root
+
+            gate = total(c * 2 * units)
+            up = total(c * 2 * units + units)
+            value = gate / (1.0 + jnp.exp(-gate)) * up
+            rows = pl.ds(pl.multiple_of(i * step, step), step)
+            out[c, x, y, rows, :] = value.astype(jnp.bfloat16)
+
+    upper, lower = pl.ds(0, units // 2), pl.ds(units // 2, units // 2)
+    two, rest = pl.ds(0, 2), pl.ds(2, 2)
+
+    def piece_a(phase):
+        if phase == 0:
+            return (
+                lambda i: out.at[0, i, y],
+                lambda i: out.at[0, i, y, upper],
+                lambda i: out.at[0, i, y, lower],
+                x,
+                along_x(y),
+            )
+        return (
+            lambda i: out.at[0, :, i],
+            lambda i: out.at[0, two, i],
+            lambda i: out.at[0, rest, i],
+            y,
+            along_y(x),
+        )
+
+    def piece_b(phase):
+        if phase == 0:
+            return (
+                lambda i: out.at[1, x, i],
+                lambda i: out.at[1, x, i, upper],
+                lambda i: out.at[1, x, i, lower],
+                y,
+                along_y(x),
+            )
+        return (
+            lambda i: out.at[1, i],
+            lambda i: out.at[1, i, two],
+            lambda i: out.at[1, i, rest],
+            x,
+            along_x(y),
+        )
+
+    two_rings(send, piece_a, piece_b)
+    send.finish()
+
+
+def sum_and_gather_hidden(part, squares):
+    _, rows, tokens = part.shape
+    out = jax.ShapeDtypeStruct((2, 4, 4, rows // 4, tokens), jnp.bfloat16)
+    scratch = [
+        pltpu.VMEM((2, rows, tokens), jnp.bfloat16),
+        pltpu.VMEM((2, 8, tokens), jnp.float32),
+        pltpu.VMEM((rows, tokens), jnp.bfloat16),
+        pltpu.VMEM((8, tokens), jnp.float32),
+        pltpu.VMEM((rows, tokens), jnp.bfloat16),
+        pltpu.VMEM((8, tokens), jnp.float32),
+    ]
+    return remote_call(hidden_kernel, out, 23, 1, scratch)(part, squares)
+
+
+def acts_kernel(part, out, landed, send_sem, recv_sem):
+    m, d = lax.axis_index("mp"), lax.axis_index("dp")
+    zh, core = d // 2, d % 2
+    z = zh * 4 + m
+    mates = [{"mp": (m + k) % 4} for k in range(1, 4)]
+
+    def at(chip):
+        return {"mp": chip % 4, "dp": (chip // 4) * 2 + core}
+
+    right, left = at((z + 1) % 8), at((z + 7) % 8)
+    sibling = {"dp": zh * 2 + 1 - core}
+    greet(mates + [right, left, sibling])
+    send = Sender(send_sem, recv_sem)
+    sums = [send(part.at[(m + k) % 4], landed.at[k - 1], mates[k - 1]) for k in range(1, 4)]
+    for copy in sums:
+        copy.wait_recv()
+
+    for c in range(2):
+        total = part[m, c].astype(jnp.float32)
+        for k in range(3):
+            total += landed[k, c].astype(jnp.float32)
+        out[c, core * 8 + z] = total.astype(jnp.bfloat16)
+
+    def block(chip):
+        return out.at[:, core * 8 + chip]
+
+    from_left = send(block(z), block(z), right)
+    from_right = send(block(z), block(z), left)
+    shared = [send(block(z), block(z), sibling)]
+    for k in range(1, 4):
+        before, after = (z + 8 - k) % 8, (z + k) % 8
+        from_left.wait_recv()
+        if k < 3:
+            next_left = send(block(before), block(before), right)
+        else:
+            piece = out.at[0, core * 8 + before]
+            next_left = send(piece, piece, right)
+        from_right.wait_recv()
+        if k < 3:
+            next_right = send(block(after), block(after), left)
+        else:
+            piece = out.at[1, core * 8 + after]
+            next_right = send(piece, piece, left)
+        shared.append(send(block(before), block(before), sibling))
+        shared.append(send(block(after), block(after), sibling))
+        from_left, from_right = next_left, next_right
+    from_left.wait_recv()
+    from_right.wait_recv()
+    far = (z + 4) % 8
+    shared.append(send(block(far), block(far), sibling))
+    for copy in shared:
+        copy.wait_recv()
+    send.finish()
+
+
+def sum_and_gather_acts(part):
+    _, copies, rows, features = part.shape
+    out = jax.ShapeDtypeStruct((copies, 16, rows, features), jnp.bfloat16)
+    scratch = [pltpu.VMEM((3, copies, rows, features), jnp.bfloat16)]
+    return remote_call(acts_kernel, out, 19, 2, scratch)(part)
+
+
+def rows_kernel(part, out, landed, send_sem, recv_sem):
+    t = lax.axis_index("tensor")
+    x, y = grid_place()
+    m, d = lax.axis_index("mp"), lax.axis_index("dp")
+    zh, core = d // 2, d % 2
+    z = zh * 4 + m
+    width = part.shape[3] // 2
+
+    def column(index):
+        return pl.ds(pl.multiple_of((index % 2) * width, 128), width)
+
+    peers = [{"tensor": (t + k) % 16} for k in range(1, 16)]
+
+    def at(chip):
+        return {"mp": chip % 4, "dp": (chip // 4) * 2 + core}
+
+    chips = [at((z + k) % 8) for k in range(1, 8)]
+    sibling = {"dp": zh * 2 + 1 - core}
+    greet(peers + chips + [sibling])
+    send = Sender(send_sem, recv_sem)
+    sums = []
+    for k in range(1, 16):
+        u = (t + k) % 16
+        source = part.at[u // 4, (u % 4) // 2, :, column(u)]
+        sums.append(send(source, landed.at[k - 1], peers[k - 1]))
+    total = part[x, y // 2, :, column(y)]
+    for k in range(15):
+        sums[k].wait_recv()
+        total += landed[k]
+    mine = core * 8 + z
+    out[mine, x, y // 2, :, column(y)] = total
+    own = out.at[mine, x, y // 2, :, column(y)]
+    spread = [send(own, own, chip) for chip in chips]
+    for copy in spread:
+        copy.wait_recv()
+
+    low, high = pl.ds(core * 8, 4), pl.ds(core * 8 + 4, 4)
+    low_a, low_b = pl.ds(core * 8, 2), pl.ds(core * 8 + 2, 2)
+    high_a, high_b = pl.ds(core * 8 + 4, 2), pl.ds(core * 8 + 6, 2)
+    two, rest = pl.ds(0, 2), pl.ds(2, 2)
+
+    def cell(members, i, j):
+        return out.at[members, i, j // 2, :, column(j)]
+
+    def piece_a(phase):
+        if phase == 0:
+            return (
+                lambda i: cell(low, i, y),
+                lambda i: cell(low_a, i, y),
+                lambda i: cell(low_b, i, y),
+                x,
+                along_x(y),
+            )
+        return (
+            lambda j: cell(low, slice(None), j),
+            lambda j: cell(low, two, j),
+            lambda j: cell(low, rest, j),
+            y,
+            along_y(x),
+        )
+
+    def piece_b(phase):
+        if phase == 0:
+            return (
+                lambda j: cell(high, x, j),
+                lambda j: cell(high_a, x, j),
+                lambda j: cell(high_b, x, j),
+                y,
+                along_y(x),
+            )
+        return (
+            lambda i: out.at[high, i],
+            lambda i: out.at[high_a, i],
+            lambda i: out.at[high_b, i],
+            x,
+            along_x(y),
+        )
+
+    two_rings(send, piece_a, piece_b)
+    half = out.at[pl.ds(core * 8, 8)]
+    last = send(half, half, sibling)
+    last.wait_recv()
+    send.finish()
+
+
+def sum_and_gather_rows(part):
+    rows, width = part.shape
+    out = jax.ShapeDtypeStruct((16, 4, 2, rows // 8, width), jnp.float32)
+    scratch = [pltpu.VMEM((15, rows // 8, width // 2), jnp.float32)]
+    full = remote_call(rows_kernel, out, 39, 3, scratch)(part.reshape(4, 2, rows // 8, width))
+    return full.reshape(16 * rows, width)
+
+
+def against(left, right, dims):
+    return lax.dot_general(left, right, (dims, ((), ())), preferred_element_type=jnp.float32)
 
 
 def on_device(tokens, norm_gain, gate_weight, up_weight, down_weight, sketch):
     feature_count = tokens.shape[1]
     offset = lax.axis_index("dp") * feature_count
     local_gain = lax.dynamic_slice_in_dim(norm_gain, offset, feature_count, 1)
-    gathered = lax.all_gather(tokens, ("mp", "tensor"), axis=0, tiled=True)
+    gathered = gather_tokens(tokens).reshape(-1, feature_count)
+    count = gathered.shape[0]
+    share_dp = lax.axis_size("dp")
     values = gathered.astype(jnp.float32)
-    square_total = lax.psum(jnp.sum(values * values, axis=1), "dp")
-    inverse_root = lax.rsqrt(square_total / D + EPSILON)
-    normed = (values[None, :, :] * inverse_root[None, :, None] * local_gain[:, None, :]).astype(
-        jnp.bfloat16
+    squares = jnp.sum(values * values, axis=1).reshape(share_dp, 1, count // share_dp)
+    squares = jnp.broadcast_to(squares, (share_dp, 8, count // share_dp))
+    parts = []
+    for c in range(2):
+        scaled = (values * local_gain[c]).astype(jnp.bfloat16)
+        for weight in (gate_weight[c], up_weight[c]):
+            parts.append(against(weight, scaled, ((0,), (1,))).astype(jnp.bfloat16))
+    part = jnp.concatenate(parts, axis=0)
+    part = part.reshape(part.shape[0], share_dp, -1).swapaxes(0, 1)
+    hidden = sum_and_gather_hidden(part, squares)
+    hidden = hidden.reshape(2, -1, hidden.shape[-1])
+    partial_out = jnp.stack(
+        [
+            against(hidden[c], down_weight[c], ((0,), (0,))).astype(jnp.bfloat16)
+            for c in range(2)
+        ],
+        axis=1,
     )
-    summed = lax.psum_scatter(
-        project_block(normed, gate_weight, up_weight).astype(jnp.bfloat16),
-        "dp",
-        scatter_dimension=0,
-        tiled=True,
-    ).astype(jnp.float32)
-    hidden = (jax.nn.silu(summed[:, :, 0]) * summed[:, :, 1]).astype(jnp.bfloat16)
-    partial_out = jnp.einsum(
-        "rch,chd->crd",
-        lax.all_gather(hidden, "tensor", axis=2, tiled=True),
-        down_weight,
-        preferred_element_type=jnp.float32,
-    )
-    layer_out = lax.psum_scatter(partial_out, "mp", scatter_dimension=1, tiled=True)
-    mine = layer_out.astype(jnp.bfloat16)
-    acts = lax.all_gather(mine, ("dp", "mp"), axis=1, tiled=True)
-
-    def against(left, right, dims):
-        return lax.dot_general(left, right, (dims, ((), ())), preferred_element_type=jnp.float32)
-
+    share_mp = lax.axis_size("mp")
+    partial_out = partial_out.reshape(share_mp, -1, 2, partial_out.shape[-1]).swapaxes(1, 2)
+    blocks = sum_and_gather_acts(partial_out)
+    acts = blocks.reshape(2, count, -1)
+    d = lax.axis_index("dp")
+    index = (d % 2) * 8 + (d // 2) * 4 + lax.axis_index("mp")
+    mine = lax.dynamic_index_in_dim(blocks, index, 1, keepdims=False)
     rows = jnp.concatenate(
         [
             against(mine[0], acts[0], ((1,), (1,))),
@@ -172,9 +594,7 @@
         ],
         axis=1,
     )
-    rows = lax.psum(rows, "tensor")
-    full = lax.all_gather(rows, ("dp", "mp"), axis=0, tiled=True)
-    count = acts.shape[1]
+    full = sum_and_gather_rows(rows)
     gram0, gram1, z = full[:, :count], full[:, count : 2 * count], full[:, 2 * count :]
     high, low = sketch_call(gram0, gram1, z)
     share = high.shape[1] // lax.axis_size(("mp", "dp"))

time: 1170 us -> 509 us (0.44)
  waiting for transfers between devices: 788 us -> 0 us
  Pallas kernels: 246 us -> 449 us
  blocking collectives: 50.9 us -> 0 us
  between operations: 14.5 us -> 1.12 us
    all_gather x4 -> x0, waiting for transfers between devices: 608 us -> none  [the longest x1 317 us: on_device(): gathered = lax.all_gather(tokens, ('mp', 'tensor'), axis=0, tiled=True)]
    pallas_call x0 -> x4, Pallas kernels: none -> 202 us  [the longest x1 70.3 us: sum_and_gather_rows(): remote_call(rows_kernel, out, 39, 3, scratch)]
    psum x1 -> x0, waiting for transfers between devices: 93.7 us -> none  [on_device(): rows = lax.psum(rows, 'tensor')]
    reduce_scatter x2 -> x0, waiting for transfers between devices: 84.8 us -> none  [the longest x1 52.8 us: on_device(): lax.psum_scatter(project_block(normed, gate_weight, up_weight).astype(jnp...]
    psum x1 -> x0, blocking collectives: 50.9 us -> none  [on_device(): square_total = lax.psum(jnp.sum(values * values, axis=1), 'dp')]
    dot_general x3 -> x0, matrix products: 19.7 us -> none  [the longest x1 7.28 us: on_device(): jnp.einsum('rch,chd->crd', lax.all_gather(hidden, 'tensor', axis=2, tiled...]
  transfers between devices with their start and end apart: 7 -> 0, of which waited for: 7 -> 0; matrix products, arithmetic and copies ran while one was open for 0% -> 0% of each run, Pallas kernels for 0% -> 0%
where the time goes in v2:
time: 509 us; the launch traced here: 503 us
  Pallas kernels  449 us (88%)
  matrix products  27.3 us (5%)
  local copies, waits for them, and re-layouts  20.8 us (4%)
    pallas_call x1, Pallas kernels, sketch_call(): pl.pallas_call(sketch_kernel, out_shape=(jax.ShapeDtypeStruct((tokens, ra...  247 us
    pallas_call x1, Pallas kernels, sum_and_gather_rows(): remote_call(rows_kernel, out, 39, 3, scratch)  70.3 us
    pallas_call x1, Pallas kernels, sum_and_gather_hidden(): return remote_call(hidden_kernel, out, 23, 1, scratch)(part, squares)  59.1 us
    pallas_call x1, Pallas kernels, sum_and_gather_acts(): return remote_call(acts_kernel, out, 19, 2, scratch)(part)  36.7 us
    pallas_call x1, Pallas kernels, gather_tokens(): return remote_call(tokens_kernel, out, 19, 0)(tokens)  36.3 us
    dot_general x13, matrix products, against(): lax.dot_general(left, right, (dims, ((), ())), preferred_element_type=jnp...  18.4 us

profile of v2, /device:TPU:1, one launch (start us, length us, event | category | flops | bytes accessed | tf_op | source)
XLA Modules:
  0.0 502.7 jit_solution(17966490953799537865)
XLA Ops:
  0.7 0.9 constant_dynamic-slice_fusion
  1.6 0.8 copy-done.1
  2.4 36.3 %shard_map.77 = bf16[4,4,64,2048]{3,2,1,0:T(8,128)(2,1)S(1)} custom-call(bf16[16,2048]{1,0:T(8,128)(2,1)S(1)} %copy-done.1), custom_call_target="tpu_custom_call" | custom-call | tf_op jit(solution)/shard_map/pallas_call | solution.py:281
  38.7 4.1 fusion.2
  42.9 3.8 fusion.13
  47.0 1.4 fusion.12
  49.1 1.5 fusion.11
  50.6 1.4 fusion.10
  52.2 2.5 copy.8
  54.7 2.7 copy.9
  57.4 59.1 %shard_map.78 = bf16[2,4,4,224,256]{4,3,2,1,0:T(8,128)(2,1)S(1)} custom-call(bf16[4,896,256]{2,1,0:T(8,128)(2,1)S(1)} %bitcast.66, f32[4,8,256]{2,1,0:T(8,128)S(1)} %broadcast_in_dim.8.squares), custom_call_target="tpu_custom_call" | custom-call | tf_op jit(solution)/shard_map/pallas_call | solution.py:394
  116.8 3.3 fusion.14
  120.9 1.1 fusion.17
  122.1 36.7 %shard_map.79 = bf16[2,16,64,512]{3,2,1,0:T(8,128)(2,1)S(1)} custom-call(bf16[4,2,64,512]{3,2,1,0:T(8,128)(2,1)S(1)} %maximum_bitcast_fusion.part), custom_call_target="tpu_custom_call" | custom-call | tf_op jit(solution)/shard_map/pallas_call | solution.py:456
  160.2 70.3 %shard_map.80 = f32[16,4,2,8,2560]{4,3,2,1,0:T(8,128)} custom-call(f32[4,2,8,2560]{3,2,1,0:T(8,128)S(1)} %bitcast.67), custom_call_target="tpu_custom_call" | custom-call | tf_op jit(solution)/shard_map/pallas_call | solution.py:548
  230.4 3.1 slice.81.z_ref
  233.5 8.4 %fusion.59 = (f32[1024,1024]{1,0:T(8,128)}, f32[1024,1024]{1,0:T(8,128)}) fusion(f32[1024,2560]{1,0:T(8,128)} %bitcast.69), kind=kLoop, calls=%fused_computation.72 | loop fusion | bytes 16777216 | tf_op jit(solution)/shard_map/slice | solution.py:598
  242.0 246.7 %shard_map.81 = (bf16[1024,512]{1,0:T(8,128)(2,1)}, bf16[1024,512]{1,0:T(8,128)(2,1)}) custom-call(f32[1024,1024]{1,0:T(8,128)} %get-tuple-element.7.g0_ref, f32[1024,1024]{1,0:T(8,128)} %get-tuple-element.6.g1_ref, f32[1024,512]{1,0:T(8,128)} %slice.81.z_ref), custom_call_target="tpu_custom_call" | custom-call | tf_op jit(solution)/shard_map/pallas_call | solution.py:111
  488.7 1.5 fusion.37
  490.2 2.1 convolution_add_fusion.1
  492.2 3.0 fusion.31
  495.3 3.0 fusion.35
  498.2 3.0 fusion.22
  501.5 0.9 convolution_add_fusion
  (29 shorter events, 3.9 us)
Async XLA Ops:
  0.6 158.2 %copy-start = (bf16[512,512]{1,0:T(8,128)(2,1)S(1)}, bf16[512,512]{1,0:T(8,128)(2,1)}, u32[]{:S(2)}) copy-start(bf16[512,512]{1,0:T(8,128)(2,1)} %param.11) | copy-start | bytes 1572868
  1.6 0.8 copy-start.1
  38.7 4.2 copy-start.5
  42.9 3.8 copy-start.3
  42.9 4.0 copy-start.6
  46.9 2.2 copy-start.2
  116.6 3.6 slice-start
  116.8 4.1 slice-start.1
  488.7 6.6 %copy-start.4 = (bf16[1024,512]{1,0:T(8,128)(2,1)S(1)}, bf16[1024,512]{1,0:T(8,128)(2,1)}, u32[]{:S(2)}) copy-start(bf16[1024,512]{1,0:T(8,128)(2,1)} %get-tuple-element.4) | copy-start | bytes 3145732

commit v3 on v2

--- a/solution.py
+++ b/solution.py
@@ -25,93 +25,124 @@
     return dot(a, b) + (dot(a, b_low) + dot(a_low, b))
 
 
+def reciprocal(value):
+    return 1.0 / value
+
+
 def inverse_factor(rows):
     lane = lax.broadcasted_iota(jnp.int32, (8, BLOCK), 1)
     sub = lax.broadcasted_iota(jnp.int32, (8, BLOCK), 0)
     rows = list(rows)
-    for j in range(BLOCK):
-        g, s = divmod(j, 8)
-        at_j = lane == j
-        below = sub > s
-        row = rows[g][s : s + 1, :]
-        inv = 1.0 / row[:, j : j + 1]
-        scaled = jnp.where(at_j, 1.0, jnp.broadcast_to(row, (8, BLOCK))) * inv
-        for h in range(g, BLOCK // 8):
-            old = rows[h]
-            col = jnp.broadcast_to(old[:, j : j + 1], (8, BLOCK))
-            if h == g:
-                new = jnp.where(at_j, 0.0, old) - col * scaled
-                rows[h] = jnp.where(below, new, old)
-            else:
-                rows[h] = jnp.where(at_j, 0.0, old) - col * scaled
+    groups = BLOCK // 8
+
+    def spread(value):
+        return jnp.broadcast_to(value, (8, BLOCK))
+
     out = []
-    for g in range(BLOCK // 8):
-        row_index = sub + 8 * g
-        pivot = jnp.sum(jnp.where(lane == row_index, rows[g], 0.0), axis=1, keepdims=True)
-        unit = jnp.where(lane == row_index, 1.0, jnp.where(lane < row_index, rows[g], 0.0))
-        out.append(unit * lax.rsqrt(pivot))
+    for g in range(groups):
+        own = (lane >= 8 * g) & (lane < 8 * g + 8)
+        cols = [[spread(rows[h][:, 8 * g + k : 8 * g + k + 1]) for k in range(8)] for h in range(g, groups)]
+        s = [[spread(cols[0][k][i : i + 1, :]) for k in range(i + 1)] for i in range(8)]
+        lines = [
+            jnp.where(own, (lane == 8 * g + k).astype(jnp.float32), spread(rows[g][k : k + 1, :]))
+            for k in range(8)
+        ]
+        factor = [[None] * 8 for _ in range(8)]
+        inv = [None] * 8
+        for k in range(8):
+            inv[k] = reciprocal(s[k][k])
+            for i in range(k + 1, 8):
+                factor[i][k] = s[i][k] * inv[k]
+            for i in range(k + 1, 8):
+                for n in range(k + 1, i + 1):
+                    s[i][n] = s[i][n] - factor[i][k] * s[n][k]
+        for k in range(8):
+            for i in range(k + 1, 8):
+                lines[i] = lines[i] - factor[i][k] * lines[k]
+        solved = [lines[k] * inv[k] for k in range(8)]
+        for i in range(7, 0, -1):
+            for k in range(i):
+                solved[k] = solved[k] - factor[i][k] * solved[i]
+        for h in range(g + 1, groups):
+            value = jnp.where(own, 0.0, rows[h])
+            c = cols[h - g]
+            first = (c[0] * solved[0] + c[1] * solved[1]) + (c[2] * solved[2] + c[3] * solved[3])
+            second = (c[4] * solved[4] + c[5] * solved[5]) + (c[6] * solved[6] + c[7] * solved[7])
+            rows[h] = value - (first + second)
+        row = lines[0] * jnp.sqrt(inv[0])
+        for k in range(1, 8):
+            row = jnp.where(sub == k, lines[k] * jnp.sqrt(inv[k]), row)
+        out.append(jnp.where(lane <= sub + 8 * g, row, 0.0))
     return jnp.concatenate(out, axis=0)
 
 
 def orth_factor(gram, low_inv):
-    n = gram.shape[0] // BLOCK
+    n = gram.shape[0]
     low_inv[...] = jnp.zeros_like(low_inv)
-
-    def step(k, carry):
-        base = pl.multiple_of(k * BLOCK, BLOCK)
-        here = pl.ds(base, BLOCK)
-        rows = [gram[pl.ds(pl.multiple_of(base + 8 * g, 8), 8), here] for g in range(BLOCK // 8)]
-        inv = inverse_factor(rows)
+    for base in range(0, n, BLOCK):
+        end = base + BLOCK
+        here, rest = pl.ds(base, BLOCK), pl.ds(end, n - end)
+        inv = inverse_factor([gram[pl.ds(base + 8 * g, 8), here] for g in range(BLOCK // 8)])
         inv_s = split(inv)
-        panel = mul(inv_s, split(gram[here, :]))
-        lane = lax.broadcasted_iota(jnp.int32, panel.shape, 1)
-        panel = jnp.where(lane >= base + BLOCK, panel, 0.0)
         low_inv[here, here] = inv
-        done = mul(inv_s, split(low_inv[here, :] * jnp.where(lane < base, 1.0, 0.0)))
-        mine = jnp.where(lane < base, done, low_inv[here, :])
-        low_inv[here, :] = mine
-        panel_s = split(panel)
-        gram[...] -= mul(panel_s, panel_s, ((0,), (0,)))
-        low_inv[...] -= mul(panel_s, split(mine), ((0,), (0,)))
-        return carry
-
-    lax.fori_loop(0, n, step, 0)
-
-
-def sketch_kernel(g0_ref, g1_ref, z_ref, out_ref, low_ref, gram, low_inv, high_z, low_z):
-    tokens, rank = z_ref.shape
-
-    def rank_step(which, g_ref):
-        g_s = split(g_ref[...])
-        z_s = split(z_ref[...]) if which == 0 else (high_z[...], low_z[...])
+        if base:
+            before = pl.ds(0, base)
+            low_inv[here, before] = mul(inv_s, split(low_inv[here, before]))
+        if end < n:
+            panel_s = split(mul(inv_s, split(gram[here, rest])))
+            gram[rest, rest] -= mul(panel_s, panel_s, ((0,), (0,)))
+            so_far = pl.ds(0, end)
+            low_inv[rest, so_far] -= mul(panel_s, split(low_inv[here, so_far]), ((0,), (0,)))
+
+
+def sketch_kernel(full, acts, basis_out, last_out, gram, low_inv, high_z, low_z):
+    tokens = full.shape[0]
+    rank = gram.shape[0]
+    share = basis_out.shape[0]
+    high, low = split(full[:, pl.ds(2 * tokens, rank)])
+    high_z[...] = high
+    low_z[...] = low
+
+    def step(n, carry):
+        g_s = split(full[:, pl.ds(pl.multiple_of((n % 2) * tokens, 128), tokens)])
+        z_s = (high_z[...], low_z[...])
         h = mul(g_s, z_s)
         gram[...] = mul(z_s, split(h), ((0,), (0,))) * (2.0**-33)
         orth_factor(gram, low_inv)
-        return h, z_s
-
-    def advance(h):
-        z = mul(split(h * (1.0 / 1024)), split(low_inv[...]), ((1,), (1,)))
-        high, low = split(z)
-        high_z[...] = high
-        low_z[...] = low
-
-    h, _ = rank_step(0, g0_ref)
-    advance(h)
-    h, _ = rank_step(1, g1_ref)
-    advance(h)
-    _, z_s = rank_step(2, g0_ref)
-    basis = mul(z_s, split(low_inv[...]), ((1,), (1,))) * (1.0 / 1024)
-    high, low = split(basis)
-    out_ref[...] = high
-    low_ref[...] = low
-
-
-def sketch_call(gram0, gram1, z):
-    tokens, rank = z.shape
+
+        @pl.when(n < 2)
+        def _():
+            high, low = split(mul(split(h * (1.0 / 1024)), split(low_inv[...]), ((1,), (1,))))
+            high_z[...] = high
+            low_z[...] = low
+
+        return carry
+
+    lax.fori_loop(0, 3, step, 0)
+    index = lax.axis_index("mp") * 4 + lax.axis_index("dp")
+    rows = low_inv[pl.ds(pl.multiple_of(index * share, share), share), :]
+    coeff = split(mul(split(rows), (high_z[...], low_z[...]), ((1,), (1,))) * (1.0 / 1024))
+    last = split(mul(coeff, split(full[:, pl.ds(0, tokens)])) * (1.0 / 1024))
+
+    def apply(pair, c):
+        def dot(a):
+            return jnp.dot(a, acts[c], preferred_element_type=jnp.float32)
+
+        return dot(pair[0]) + dot(pair[1])
+
+    basis_out[...] = apply(coeff, 0)
+    last_out[...] = apply(last, 1)
+
+
+def sketch_call(full, acts):
+    tokens = full.shape[0]
+    rank = full.shape[1] - 2 * tokens
+    features = acts.shape[2]
+    shape = jax.ShapeDtypeStruct((rank // 16, features), jnp.float32)
     return pl.pallas_call(
         sketch_kernel,
-        out_shape=(jax.ShapeDtypeStruct((tokens, rank), jnp.bfloat16),) * 2,
-        in_specs=[pl.BlockSpec(memory_space=pltpu.VMEM)] * 3,
+        out_shape=(shape, shape),
+        in_specs=[pl.BlockSpec(memory_space=pltpu.VMEM)] * 2,
         out_specs=(pl.BlockSpec(memory_space=pltpu.VMEM),) * 2,
         scratch_shapes=[
             pltpu.VMEM((rank, rank), jnp.float32),
@@ -120,7 +151,7 @@
             pltpu.VMEM((tokens, rank), jnp.bfloat16),
         ],
         compiler_params=pltpu.CompilerParams(vmem_limit_bytes=56 * 2**20),
-    )(gram0, gram1, z)
+    )(full, acts)
 
 
 MESH = pl.DeviceIdType.MESH
@@ -288,17 +319,21 @@
     sibling, partner = {"dp": z * 2 + 1 - core}, {"dp": (1 - z) * 2 + core}
     greet([sibling, partner] + xy_neighbours(x, y))
     send = Sender(send_sem, recv_sem)
-    other, mine = (1 - z) * 2, z * 2
-    there = 1 - core
-    first = send(part.at[other + there], near.at[1], sibling)
-    first_sq = send(squares.at[other + there], near_sq.at[1], sibling)
-    second = send(part.at[mine + there], near.at[0], sibling)
-    second_sq = send(squares.at[mine + there], near_sq.at[0], sibling)
-    units = out.shape[3]
+    units, tokens = out.shape[3], out.shape[4]
     step = 32
 
+    def share(zh, side):
+        return pl.ds(pl.multiple_of((zh * 2 + side) * tokens, 128), tokens)
+
+    far_near, far_mine = share(1 - z, 1 - core), share(1 - z, core)
+    own_near, own = share(z, 1 - core), share(z, core)
+    first = send(part.at[:, far_near], near.at[1], sibling)
+    first_sq = send(squares.at[:, far_near], near_sq.at[1], sibling)
+    second = send(part.at[:, own_near], near.at[0], sibling)
+    second_sq = send(squares.at[:, own_near], near_sq.at[0], sibling)
+
     first_sq.wait_recv()
-    pair_sq[...] = squares[other + core] + near_sq[1]
+    pair_sq[...] = squares[:, far_mine] + near_sq[1]
     across_sq = send(pair_sq, far_sq, partner)
     first.wait_recv()
     across = []
@@ -307,7 +342,7 @@
         @pl.loop(0, 2 * units // step)
         def _(i):
             rows = pl.ds(pl.multiple_of(c * 2 * units + i * step, step), step)
-            total = part[other + core, rows, :].astype(jnp.float32) + near[1, rows, :].astype(
+            total = part[rows, far_mine].astype(jnp.float32) + near[1, rows, :].astype(
                 jnp.float32
             )
             pair[rows, :] = total.astype(jnp.bfloat16)
@@ -317,7 +352,7 @@
 
     second_sq.wait_recv()
     across_sq.wait_recv()
-    square_total = squares[mine + core] + near_sq[0] + far_sq[...]
+    square_total = squares[:, own] + near_sq[0] + far_sq[...]
     root = lax.rsqrt(square_total[0:1, :] / D + EPSILON)
     second.wait_recv()
     for c in range(2):
@@ -328,7 +363,7 @@
             def total(row):
                 rows = pl.ds(pl.multiple_of(row + i * step, step), step)
                 return (
-                    part[mine + core, rows, :].astype(jnp.float32)
+                    part[rows, own].astype(jnp.float32)
                     + near[0, rows, :].astype(jnp.float32)
                     + far[rows, :].astype(jnp.float32)
                 ) * root
@@ -381,7 +416,7 @@
 
 
 def sum_and_gather_hidden(part, squares):
-    _, rows, tokens = part.shape
+    rows, tokens = part.shape[0], part.shape[1] // lax.axis_size("dp")
     out = jax.ShapeDtypeStruct((2, 4, 4, rows // 4, tokens), jnp.bfloat16)
     scratch = [
         pltpu.VMEM((2, rows, tokens), jnp.bfloat16),
@@ -559,17 +594,14 @@
     local_gain = lax.dynamic_slice_in_dim(norm_gain, offset, feature_count, 1)
     gathered = gather_tokens(tokens).reshape(-1, feature_count)
     count = gathered.shape[0]
-    share_dp = lax.axis_size("dp")
     values = gathered.astype(jnp.float32)
-    squares = jnp.sum(values * values, axis=1).reshape(share_dp, 1, count // share_dp)
-    squares = jnp.broadcast_to(squares, (share_dp, 8, count // share_dp))
+    squares = jnp.broadcast_to(jnp.sum(values * values, axis=1), (8, count))
     parts = []
     for c in range(2):
         scaled = (values * local_gain[c]).astype(jnp.bfloat16)
         for weight in (gate_weight[c], up_weight[c]):
             parts.append(against(weight, scaled, ((0,), (1,))).astype(jnp.bfloat16))
     part = jnp.concatenate(parts, axis=0)
-    part = part.reshape(part.shape[0], share_dp, -1).swapaxes(0, 1)
     hidden = sum_and_gather_hidden(part, squares)
     hidden = hidden.reshape(2, -1, hidden.shape[-1])
     partial_out = jnp.stack(
@@ -595,19 +627,8 @@
         axis=1,
     )
     full = sum_and_gather_rows(rows)
-    gram0, gram1, z = full[:, :count], full[:, count : 2 * count], full[:, 2 * count :]
-    high, low = sketch_call(gram0, gram1, z)
-    share = high.shape[1] // lax.axis_size(("mp", "dp"))
-    start = lax.axis_index(("mp", "dp")) * share
-    high = lax.dynamic_slice_in_dim(high, start, share, 1)
-    low = lax.dynamic_slice_in_dim(low, start, share, 1)
-    last = mul(split(gram0), (high, low)) * (1.0 / count)
-    basis_share = against(acts[0], high, ((0,), (0,))) + against(acts[0], low, ((0,), (0,)))
-    last_high, last_low = split(last)
-    projected = against(acts[1], last_high, ((0,), (0,))) + against(
-        acts[1], last_low, ((0,), (0,))
-    )
-    return (basis_share, projected)
+    basis_share, projected = sketch_call(full, acts)
+    return (basis_share.T, projected.T)
 
 
 def solution(mesh):

time: 509 us -> 316 us (0.62); the launches traced: 503 us -> 315 us
  Pallas kernels: 449 us -> 295 us
  local copies, waits for them, and re-layouts: 20.8 us -> 3.28 us
  matrix products: 27.3 us -> 11.4 us
    pallas_call x1, Pallas kernels: 247 us -> 92.8 us  [sketch_call(): pl.pallas_call(sketch_kernel, out_shape=(shape, shape), in_specs=[pl.Bloc...]
    slice x3 -> x1, local copies, waits for them, and re-layouts: 11.7 us -> 0.22 us  [on_device(): acts[0]]
    dot_general x3 -> x0, matrix products: 8.97 us -> none  [dot(): lax.dot_general(a, b, (contract, ((), ())), preferred_element_type=jnp.fl...]
    dot_general x13 -> x9, matrix products: 18.4 us -> 11.4 us  [against(): lax.dot_general(left, right, (dims, ((), ())), preferred_element_type=jnp...]
where the time goes in v3:
time: 316 us; the launch traced here: 315 us
  Pallas kernels  295 us (93%)
  matrix products  11.4 us (4%)
  other arithmetic  4.42 us (1%)
  local copies, waits for them, and re-layouts  3.28 us (1%)
    pallas_call x1, Pallas kernels, sketch_call(): pl.pallas_call(sketch_kernel, out_shape=(shape, shape), in_specs=[pl.Bloc...  92.8 us
    pallas_call x1, Pallas kernels, sum_and_gather_rows(): remote_call(rows_kernel, out, 39, 3, scratch)  70.7 us
    pallas_call x1, Pallas kernels, sum_and_gather_hidden(): return remote_call(hidden_kernel, out, 23, 1, scratch)(part, squares)  58.8 us
    pallas_call x1, Pallas kernels, sum_and_gather_acts(): return remote_call(acts_kernel, out, 19, 2, scratch)(part)  36.7 us
    pallas_call x1, Pallas kernels, gather_tokens(): return remote_call(tokens_kernel, out, 19, 0)(tokens)  36.3 us
    dot_general x9, matrix products, against(): lax.dot_general(left, right, (dims, ((), ())), preferred_element_type=jnp...  11.4 us

profile of v3, /device:TPU:1, one launch (start us, length us, event | category | flops | bytes accessed | tf_op | source)
XLA Modules:
  0.0 315.2 jit_solution(18336273426628963404)
XLA Ops:
  0.7 0.9 constant_dynamic-slice_fusion
  1.6 0.8 copy-done.2
  2.4 36.3 %shard_map.77 = bf16[4,4,64,2048]{3,2,1,0:T(8,128)(2,1)S(1)} custom-call(bf16[16,2048]{1,0:T(8,128)(2,1)S(1)} %copy-done.2), custom_call_target="tpu_custom_call" | custom-call | tf_op jit(solution)/shard_map/pallas_call | solution.py:312
  38.7 4.2 %fusion.2 = (f32[4,4,64]{2,1,0:T(4,128)S(1)}, bf16[4,4,64,2048]{3,2,1,0:T(8,128)(2,1)}, bf16[4,4,64,2048]{3,2,1,0:T(8,128)(2,1)}) fusion(bf16[4,4,64,2048]{3,2,1,0:T(8,128)(2,1)S(1)} %shard_map.77, f32[2048]{0:T(1024)S(1)} %bitcast.77, f32[2048]{0:T(1024)S(1)} %bitcast.76), kind=kLoop, calls=%fused_computation.5 | loop fusion | flops 14679040 | bytes 12603392 | tf_op jit(solution)/shard_map/reduce_sum | solution.py:598
  42.9 0.1 reduce_sum.12
  43.0 3.7 %fusion.12 = bf16[224,1024]{1,0:T(8,128)(2,1)S(1)} fusion(bf16[1024,2048]{1,0:T(8,128)(2,1)} %bitcast.68, bf16[2,2048,224]{1,2,0:T(8,128)(2,1)S(1)} %copy-done.5), kind=kOutput, calls=%fused_computation.20 | convolution fusion | flops 939753472 | bytes 5570560 | tf_op jit(solution)/shard_map/dot_general | solution.py:588
  46.7 0.3 copy-done.6
  47.0 1.5 fusion.11
  48.5 0.7 copy-done.3
  49.2 1.4 fusion.10
  50.6 1.5 fusion.9
  52.1 0.1 pad_maximum_fusion.part
  52.3 58.8 %shard_map.78 = bf16[2,4,4,224,256]{4,3,2,1,0:T(8,128)(2,1)S(1)} custom-call(bf16[896,1024]{1,0:T(8,128)(2,1)S(1)} %pad_maximum_fusion.part, f32[8,1024]{1,0:T(8,128)S(1)} %broadcast_in_dim.3.squares), custom_call_target="tpu_custom_call" | custom-call | tf_op jit(solution)/shard_map/pallas_call | solution.py:429
  111.1 0.2 fusion.33
  111.4 1.1 fusion.13
  112.5 1.1 fusion.16
  113.6 0.1 maximum_bitcast_fusion.part
  113.7 36.7 %shard_map.79 = bf16[2,16,64,512]{3,2,1,0:T(8,128)(2,1)S(1)} custom-call(bf16[4,2,64,512]{3,2,1,0:T(8,128)(2,1)S(1)} %maximum_bitcast_fusion.part), custom_call_target="tpu_custom_call" | custom-call | tf_op jit(solution)/shard_map/pallas_call | solution.py:491
  150.4 0.2 fusion.28
  150.6 0.2 fusion.34
  150.8 0.4 fusion.27
  151.3 0.4 fusion.29
  151.8 70.7 %shard_map.80 = f32[16,4,2,8,2560]{4,3,2,1,0:T(8,128)} custom-call(f32[4,2,8,2560]{3,2,1,0:T(8,128)S(1)} %bitcast.64), custom_call_target="tpu_custom_call" | custom-call | tf_op jit(solution)/shard_map/pallas_call | solution.py:583
  222.5 92.8 %shard_map.81 = (f32[32,512]{1,0:T(8,128)}, f32[32,512]{1,0:T(8,128)}) custom-call(f32[1024,2560]{1,0:T(8,128)} %bitcast.65, bf16[2,1024,512]{2,1,0:T(8,128)(2,1)} %bitcast.63), custom_call_target="tpu_custom_call" | custom-call | tf_op jit(solution)/shard_map/pallas_call | solution.py:142
  (18 shorter events, 0.1 us)
Async XLA Ops:
  0.6 149.7 %copy-start = (bf16[512,512]{1,0:T(8,128)(2,1)S(1)}, bf16[512,512]{1,0:T(8,128)(2,1)}, u32[]{:S(2)}) copy-start(bf16[512,512]{1,0:T(8,128)(2,1)} %param.11) | copy-start | bytes 1572868
  1.6 0.8 copy-start.2
  38.7 4.3 %copy-start.5 = (bf16[2,2048,224]{1,2,0:T(8,128)(2,1)S(1)}, bf16[2,2048,224]{1,2,0:T(8,128)(2,1)}, u32[]{:S(2)}) copy-start(bf16[2,2048,224]{1,2,0:T(8,128)(2,1)} %param.9) | copy-start | bytes 5505028
  43.0 3.8 %copy-start.4 = (bf16[4,4,64,2048]{3,2,1,0:T(8,128)(2,1)S(1)}, bf16[4,4,64,2048]{3,2,1,0:T(8,128)(2,1)}, u32[]{:S(2)}) copy-start(bf16[4,4,64,2048]{3,2,1,0:T(8,128)(2,1)} %get-tuple-element.7) | copy-start | bytes 12582916
  43.0 4.0 %copy-start.6 = (bf16[2,2048,224]{1,2,0:T(8,128)(2,1)S(1)}, bf16[2,2048,224]{1,2,0:T(8,128)(2,1)}, u32[]{:S(2)}) copy-start(bf16[2,2048,224]{1,2,0:T(8,128)(2,1)} %param.8) | copy-start | bytes 5505028
  47.0 2.2 copy-start.3
  52.1 59.3 %slice-start = ((s8[7340032]{0:T(1024)(128)(4,1)}), s8[4194304]{0:T(1024)(128)(4,1)S(1)}, s32[]{:S(2)}) async-start(s8[7340032]{0:T(1024)(128)(4,1)} %bitcast.78), calls=%async_computation | async-start | bytes 8388608
  52.3 59.1 %slice-start.1 = ((s8[7340032]{0:T(1024)(128)(4,1)}), s8[3145728]{0:T(1024)(128)(4,1)S(1)}, s32[]{:S(2)}) async-start(s8[7340032]{0:T(1024)(128)(4,1)} %bitcast.78), calls=%async_computation.1 | async-start | bytes 6291456
  150.4 1.3 copy-start.1

commit v4 on v3

--- a/solution.py
+++ b/solution.py
@@ -41,11 +41,13 @@
     out = []
     for g in range(groups):
         own = (lane >= 8 * g) & (lane < 8 * g + 8)
-        cols = [[spread(rows[h][:, 8 * g + k : 8 * g + k + 1]) for k in range(8)] for h in range(g, groups)]
-        s = [[spread(cols[0][k][i : i + 1, :]) for k in range(i + 1)] for i in range(8)]
+        cols = [[spread(rows[h][:, 8 * g + k : 8 * g + k + 1]) for k in range(8)] for h in range(g + 1, min(g + 2, groups))]
+        plain = [spread(rows[g][k : k + 1, :]) for k in range(8)]
+        s = [
+            [spread(plain[i][:, 8 * g + k : 8 * g + k + 1]) for k in range(i + 1)] for i in range(8)
+        ]
         lines = [
-            jnp.where(own, (lane == 8 * g + k).astype(jnp.float32), spread(rows[g][k : k + 1, :]))
-            for k in range(8)
+            jnp.where(own, (lane == 8 * g + k).astype(jnp.float32), plain[k]) for k in range(8)
         ]
         factor = [[None] * 8 for _ in range(8)]
         inv = [None] * 8
@@ -63,12 +65,23 @@
         for i in range(7, 0, -1):
             for k in range(i):
                 solved[k] = solved[k] - factor[i][k] * solved[i]
-        for h in range(g + 1, groups):
+        for h in range(g + 1, min(g + 2, groups)):
             value = jnp.where(own, 0.0, rows[h])
-            c = cols[h - g]
+            c = cols[h - g - 1]
             first = (c[0] * solved[0] + c[1] * solved[1]) + (c[2] * solved[2] + c[3] * solved[3])
             second = (c[4] * solved[4] + c[5] * solved[5]) + (c[6] * solved[6] + c[7] * solved[7])
             rows[h] = value - (first + second)
+        if g + 2 < groups:
+            tight = solved[0]
+            for k in range(1, 8):
+                tight = jnp.where(sub == k, solved[k], tight)
+            zero = jnp.zeros_like(tight)
+            wide = jnp.concatenate([tight if n == g else zero for n in range(groups)], axis=0)
+            tall = jnp.concatenate(rows[g + 2 :], axis=0)
+            change = mul(split(tall), split(wide))
+            for h in range(g + 2, groups):
+                n = 8 * (h - g - 2)
+                rows[h] = jnp.where(own, 0.0, rows[h]) - change[n : n + 8, :]
         row = lines[0] * jnp.sqrt(inv[0])
         for k in range(1, 8):
             row = jnp.where(sub == k, lines[k] * jnp.sqrt(inv[k]), row)
@@ -78,21 +91,38 @@
 
 def orth_factor(gram, low_inv):
     n = gram.shape[0]
+    blocks = n // BLOCK
     low_inv[...] = jnp.zeros_like(low_inv)
-    for base in range(0, n, BLOCK):
-        end = base + BLOCK
-        here, rest = pl.ds(base, BLOCK), pl.ds(end, n - end)
-        inv = inverse_factor([gram[pl.ds(base + 8 * g, 8), here] for g in range(BLOCK // 8)])
+    at = [pl.ds(k * BLOCK, BLOCK) for k in range(blocks)]
+
+    def diagonal(k):
+        return [gram[pl.ds(k * BLOCK + 8 * g, 8), at[k]] for g in range(BLOCK // 8)]
+
+    inv = inverse_factor(diagonal(0))
+    for k in range(blocks):
         inv_s = split(inv)
-        low_inv[here, here] = inv
-        if base:
-            before = pl.ds(0, base)
-            low_inv[here, before] = mul(inv_s, split(low_inv[here, before]))
-        if end < n:
-            panel_s = split(mul(inv_s, split(gram[here, rest])))
-            gram[rest, rest] -= mul(panel_s, panel_s, ((0,), (0,)))
-            so_far = pl.ds(0, end)
-            low_inv[rest, so_far] -= mul(panel_s, split(low_inv[here, so_far]), ((0,), (0,)))
+        low_inv[at[k], at[k]] = inv
+        panel = {}
+        if k + 1 < blocks:
+            panel[k + 1] = split(mul(inv_s, split(gram[at[k], at[k + 1]])))
+            gram[at[k + 1], at[k + 1]] -= mul(panel[k + 1], panel[k + 1], ((0,), (0,)))
+            following = inverse_factor(diagonal(k + 1))
+        if k:
+            before = pl.ds(0, k * BLOCK)
+            low_inv[at[k], before] = mul(inv_s, split(low_inv[at[k], before]))
+        so_far = pl.ds(0, (k + 1) * BLOCK)
+        mine = split(low_inv[at[k], so_far])
+        for i in range(k + 1, blocks):
+            if i not in panel:
+                panel[i] = split(mul(inv_s, split(gram[at[k], at[i]])))
+            low_inv[at[i], so_far] -= mul(panel[i], mine, ((0,), (0,)))
+            for j in range(i, blocks):
+                if j not in panel:
+                    panel[j] = split(mul(inv_s, split(gram[at[k], at[j]])))
+                if (i, j) != (k + 1, k + 1):
+                    gram[at[i], at[j]] -= mul(panel[i], panel[j], ((0,), (0,)))
+        if k + 1 < blocks:
+            inv = following
 
 
 def sketch_kernel(full, acts, basis_out, last_out, gram, low_inv, high_z, low_z):
@@ -320,98 +350,128 @@
     greet([sibling, partner] + xy_neighbours(x, y))
     send = Sender(send_sem, recv_sem)
     units, tokens = out.shape[3], out.shape[4]
+    chunk = tokens // 2
     step = 32
 
-    def share(zh, side):
-        return pl.ds(pl.multiple_of((zh * 2 + side) * tokens, 128), tokens)
-
-    far_near, far_mine = share(1 - z, 1 - core), share(1 - z, core)
-    own_near, own = share(z, 1 - core), share(z, core)
-    first = send(part.at[:, far_near], near.at[1], sibling)
-    first_sq = send(squares.at[:, far_near], near_sq.at[1], sibling)
-    second = send(part.at[:, own_near], near.at[0], sibling)
-    second_sq = send(squares.at[:, own_near], near_sq.at[0], sibling)
+    def share(zh, side, h=None):
+        start = (zh * 2 + side) * tokens
+        if h is None:
+            return pl.ds(pl.multiple_of(start, 128), tokens)
+        return pl.ds(pl.multiple_of(start + h * chunk, 128), chunk)
+
+    first_sq = send(squares.at[:, share(1 - z, 1 - core)], near_sq.at[1], sibling)
+    first = [
+        send(part.at[:, share(1 - z, 1 - core, h)], near.at[1, h], sibling) for h in range(2)
+    ]
+    second_sq = send(squares.at[:, share(z, 1 - core)], near_sq.at[0], sibling)
+    second = [send(part.at[:, share(z, 1 - core, h)], near.at[0, h], sibling) for h in range(2)]
 
     first_sq.wait_recv()
-    pair_sq[...] = squares[:, far_mine] + near_sq[1]
+    pair_sq[...] = squares[:, share(1 - z, core)] + near_sq[1]
     across_sq = send(pair_sq, far_sq, partner)
-    first.wait_recv()
     across = []
-    for c in range(2):
-
-        @pl.loop(0, 2 * units // step)
+    for h in range(2):
+        first[h].wait_recv()
+
+        @pl.loop(0, 4 * units // step)
         def _(i):
-            rows = pl.ds(pl.multiple_of(c * 2 * units + i * step, step), step)
-            total = part[rows, far_mine].astype(jnp.float32) + near[1, rows, :].astype(
-                jnp.float32
-            )
-            pair[rows, :] = total.astype(jnp.bfloat16)
-
-        rows = pl.ds(c * 2 * units, 2 * units)
-        across.append(send(pair.at[rows], far.at[rows], partner))
+            rows = pl.ds(pl.multiple_of(i * step, step), step)
+            total = part[rows, share(1 - z, core, h)].astype(jnp.float32) + near[
+                1, h, rows, :
+            ].astype(jnp.float32)
+            pair[h, rows, :] = total.astype(jnp.bfloat16)
+
+        across.append(send(pair.at[h], far.at[h], partner))
 
     second_sq.wait_recv()
     across_sq.wait_recv()
-    square_total = squares[:, own] + near_sq[0] + far_sq[...]
+    square_total = squares[:, share(z, core)] + near_sq[0] + far_sq[...]
     root = lax.rsqrt(square_total[0:1, :] / D + EPSILON)
-    second.wait_recv()
-    for c in range(2):
-        across[c].wait_recv()
-
-        @pl.loop(0, units // step)
-        def _(i):
-            def total(row):
-                rows = pl.ds(pl.multiple_of(row + i * step, step), step)
-                return (
-                    part[rows, own].astype(jnp.float32)
-                    + near[0, rows, :].astype(jnp.float32)
-                    + far[rows, :].astype(jnp.float32)
-                ) * root
-
-            gate = total(c * 2 * units)
-            up = total(c * 2 * units + units)
-            value = gate / (1.0 + jnp.exp(-gate)) * up
-            rows = pl.ds(pl.multiple_of(i * step, step), step)
-            out[c, x, y, rows, :] = value.astype(jnp.bfloat16)
+
+    def activate(h):
+        second[h].wait_recv()
+        across[h].wait_recv()
+        lanes = pl.ds(h * chunk, chunk)
+        scale = root[:, h * chunk : (h + 1) * chunk]
+        for c in range(2):
+
+            @pl.loop(0, units // step)
+            def _(i):
+                def total(row):
+                    rows = pl.ds(pl.multiple_of(row + i * step, step), step)
+                    return (
+                        part[rows, share(z, core, h)].astype(jnp.float32)
+                        + near[0, h, rows, :].astype(jnp.float32)
+                        + far[h, rows, :].astype(jnp.float32)
+                    ) * scale
+
+                gate = total(c * 2 * units)
+                up = total(c * 2 * units + units)
+                value = gate / (1.0 + jnp.exp(-gate)) * up
+                rows = pl.ds(pl.multiple_of(i * step, step), step)
+                out[c, x, y, rows, lanes] = value.astype(jnp.bfloat16)
 
     upper, lower = pl.ds(0, units // 2), pl.ds(units // 2, units // 2)
+    every = slice(None)
     two, rest = pl.ds(0, 2), pl.ds(2, 2)
 
-    def piece_a(phase):
+    def start(h, phase):
+        lanes = pl.ds(h * chunk, chunk)
         if phase == 0:
             return (
-                lambda i: out.at[0, i, y],
-                lambda i: out.at[0, i, y, upper],
-                lambda i: out.at[0, i, y, lower],
+                ring(
+                    send,
+                    lambda i: out.at[0, i, y, :, lanes],
+                    lambda i: out.at[0, i, y, upper, lanes],
+                    lambda i: out.at[0, i, y, lower, lanes],
+                    x,
+                    along_x(y),
+                ),
+                ring(
+                    send,
+                    lambda i: out.at[1, x, i, :, lanes],
+                    lambda i: out.at[1, x, i, upper, lanes],
+                    lambda i: out.at[1, x, i, lower, lanes],
+                    y,
+                    along_y(x),
+                ),
+            )
+        return (
+            ring(
+                send,
+                lambda i: out.at[0, every, i, :, lanes],
+                lambda i: out.at[0, two, i, :, lanes],
+                lambda i: out.at[0, rest, i, :, lanes],
+                y,
+                along_y(x),
+            ),
+            ring(
+                send,
+                lambda i: out.at[1, i, every, :, lanes],
+                lambda i: out.at[1, i, two, :, lanes],
+                lambda i: out.at[1, i, rest, :, lanes],
                 x,
                 along_x(y),
-            )
-        return (
-            lambda i: out.at[0, :, i],
-            lambda i: out.at[0, two, i],
-            lambda i: out.at[0, rest, i],
-            y,
-            along_y(x),
+            ),
         )
 
-    def piece_b(phase):
-        if phase == 0:
-            return (
-                lambda i: out.at[1, x, i],
-                lambda i: out.at[1, x, i, upper],
-                lambda i: out.at[1, x, i, lower],
-                y,
-                along_y(x),
-            )
-        return (
-            lambda i: out.at[1, i],
-            lambda i: out.at[1, i, two],
-            lambda i: out.at[1, i, rest],
-            x,
-            along_x(y),
-        )
-
-    two_rings(send, piece_a, piece_b)
+    def forward(pair_of_rings):
+        return [copy for one in pair_of_rings for copy in one()]
+
+    def settle(copies):
+        for copy in copies:
+            copy.wait_recv()
+
+    activate(0)
+    rings = start(0, 0)
+    settle(forward(rings))
+    early = start(0, 1)
+    activate(1)
+    rings = start(1, 0)
+    tail = forward(early)
+    settle(forward(rings))
+    tail += forward(start(1, 1))
+    settle(tail)
     send.finish()
 
 
@@ -419,14 +479,14 @@
     rows, tokens = part.shape[0], part.shape[1] // lax.axis_size("dp")
     out = jax.ShapeDtypeStruct((2, 4, 4, rows // 4, tokens), jnp.bfloat16)
     scratch = [
-        pltpu.VMEM((2, rows, tokens), jnp.bfloat16),
+        pltpu.VMEM((2, 2, rows, tokens // 2), jnp.bfloat16),
         pltpu.VMEM((2, 8, tokens), jnp.float32),
-        pltpu.VMEM((rows, tokens), jnp.bfloat16),
+        pltpu.VMEM((2, rows, tokens // 2), jnp.bfloat16),
         pltpu.VMEM((8, tokens), jnp.float32),
-        pltpu.VMEM((rows, tokens), jnp.bfloat16),
+        pltpu.VMEM((2, rows, tokens // 2), jnp.bfloat16),
         pltpu.VMEM((8, tokens), jnp.float32),
     ]
-    return remote_call(hidden_kernel, out, 23, 1, scratch)(part, squares)
+    return remote_call(hidden_kernel, out, 41, 1, scratch)(part, squares)
 
 
 def acts_kernel(part, out, landed, send_sem, recv_sem):
@@ -569,10 +629,28 @@
             along_x(y),
         )
 
-    two_rings(send, piece_a, piece_b)
-    half = out.at[pl.ds(core * 8, 8)]
-    last = send(half, half, sibling)
-    last.wait_recv()
+    shared = []
+
+    def share(source):
+        shared.append(send(source, source, sibling))
+
+    a, b = ring(send, *piece_a(0)), ring(send, *piece_b(0))
+    for copy in [*a(), *b()]:
+        copy.wait_recv()
+    a, b = ring(send, *piece_a(1)), ring(send, *piece_b(1))
+    block_a, block_b = piece_a(1)[0], piece_b(1)[0]
+    share(block_a(y))
+    share(block_b(x))
+    pending = [*a(), *b()]
+    for side in (3, 1):
+        share(block_a((y + side) % 4))
+        share(block_b((x + side) % 4))
+    for copy in pending:
+        copy.wait_recv()
+    share(block_a((y + 2) % 4))
+    share(block_b((x + 2) % 4))
+    for copy in shared:
+        copy.wait_recv()
     send.finish()
 
 
@@ -580,7 +658,7 @@
     rows, width = part.shape
     out = jax.ShapeDtypeStruct((16, 4, 2, rows // 8, width), jnp.float32)
     scratch = [pltpu.VMEM((15, rows // 8, width // 2), jnp.float32)]
-    full = remote_call(rows_kernel, out, 39, 3, scratch)(part.reshape(4, 2, rows // 8, width))
+    full = remote_call(rows_kernel, out, 46, 3, scratch)(part.reshape(4, 2, rows // 8, width))
     return full.reshape(16 * rows, width)
 
 

time: 316 us -> 292 us (0.924)
  Pallas kernels: 295 us -> 272 us
    pallas_call x1, Pallas kernels: 92.8 us -> 73.5 us  [sketch_call(): pl.pallas_call(sketch_kernel, out_shape=(shape, shape), in_specs=[pl.Bloc...]
    pallas_call x2, Pallas kernels: 130 us -> 123 us  [the longest x1 64.9 us: sum_and_gather_rows(): remote_call(rows_kernel, out, 46, 3, scratch)]
where the time goes in v4:
time: 292 us
  Pallas kernels  272 us (93%)
  matrix products  11.4 us (4%)
  other arithmetic  4.42 us (2%)
  local copies, waits for them, and re-layouts  3.28 us (1%)
    pallas_call x1, Pallas kernels, sketch_call(): pl.pallas_call(sketch_kernel, out_shape=(shape, shape), in_specs=[pl.Bloc...  73.5 us
    pallas_call x1, Pallas kernels, sum_and_gather_rows(): remote_call(rows_kernel, out, 46, 3, scratch)  64.9 us
    pallas_call x1, Pallas kernels, sum_and_gather_hidden(): return remote_call(hidden_kernel, out, 41, 1, scratch)(part, squares)  58 us
    pallas_call x1, Pallas kernels, sum_and_gather_acts(): return remote_call(acts_kernel, out, 19, 2, scratch)(part)  39.6 us
    pallas_call x1, Pallas kernels, gather_tokens(): return remote_call(tokens_kernel, out, 19, 0)(tokens)  36.3 us
    dot_general x9, matrix products, against(): lax.dot_general(left, right, (dims, ((), ())), preferred_element_type=jnp...  11.4 us

profile of v4, /device:TPU:1, one launch (start us, length us, event | category | flops | bytes accessed | tf_op | source)
XLA Modules:
  0.0 292.3 jit_solution(15214438425879400135)
XLA Ops:
  0.7 0.9 constant_dynamic-slice_fusion
  1.6 0.8 copy-done.2
  2.4 36.3 %shard_map.77 = bf16[4,4,64,2048]{3,2,1,0:T(8,128)(2,1)S(1)} custom-call(bf16[16,2048]{1,0:T(8,128)(2,1)S(1)} %copy-done.2), custom_call_target="tpu_custom_call" | custom-call | tf_op jit(solution)/shard_map/pallas_call | solution.py:342
  38.7 4.2 %fusion.2 = (f32[4,4,64]{2,1,0:T(4,128)S(1)}, bf16[4,4,64,2048]{3,2,1,0:T(8,128)(2,1)}, bf16[4,4,64,2048]{3,2,1,0:T(8,128)(2,1)}) fusion(bf16[4,4,64,2048]{3,2,1,0:T(8,128)(2,1)S(1)} %shard_map.77, f32[2048]{0:T(1024)S(1)} %bitcast.77, f32[2048]{0:T(1024)S(1)} %bitcast.76), kind=kLoop, calls=%fused_computation.5 | loop fusion | flops 14679040 | bytes 12603392 | tf_op jit(solution)/shard_map/reduce_sum | solution.py:676
  42.9 0.1 reduce_sum.12
  43.0 3.7 %fusion.12 = bf16[224,1024]{1,0:T(8,128)(2,1)S(1)} fusion(bf16[1024,2048]{1,0:T(8,128)(2,1)} %bitcast.68, bf16[2,2048,224]{1,2,0:T(8,128)(2,1)S(1)} %copy-done.5), kind=kOutput, calls=%fused_computation.20 | convolution fusion | flops 939753472 | bytes 5570560 | tf_op jit(solution)/shard_map/dot_general | solution.py:666
  46.7 0.3 copy-done.6
  47.0 1.5 fusion.11
  48.5 0.7 copy-done.3
  49.2 1.4 fusion.10
  50.6 1.5 fusion.9
  52.1 0.1 pad_maximum_fusion.part
  52.3 58.0 %shard_map.78 = bf16[2,4,4,224,256]{4,3,2,1,0:T(8,128)(2,1)S(1)} custom-call(bf16[896,1024]{1,0:T(8,128)(2,1)S(1)} %pad_maximum_fusion.part, f32[8,1024]{1,0:T(8,128)S(1)} %broadcast_in_dim.3.squares), custom_call_target="tpu_custom_call" | custom-call | tf_op jit(solution)/shard_map/pallas_call | solution.py:489
  110.3 0.2 fusion.33
  110.6 1.1 fusion.13
  111.7 1.1 fusion.16
  112.8 0.1 maximum_bitcast_fusion.part
  112.9 39.6 %shard_map.79 = bf16[2,16,64,512]{3,2,1,0:T(8,128)(2,1)S(1)} custom-call(bf16[4,2,64,512]{3,2,1,0:T(8,128)(2,1)S(1)} %maximum_bitcast_fusion.part), custom_call_target="tpu_custom_call" | custom-call | tf_op jit(solution)/shard_map/pallas_call | solution.py:551
  152.5 0.2 fusion.28
  152.7 0.2 fusion.34
  153.0 0.4 fusion.27
  153.4 0.4 fusion.29
  153.9 64.9 %shard_map.80 = f32[16,4,2,8,2560]{4,3,2,1,0:T(8,128)} custom-call(f32[4,2,8,2560]{3,2,1,0:T(8,128)S(1)} %bitcast.64), custom_call_target="tpu_custom_call" | custom-call | tf_op jit(solution)/shard_map/pallas_call | solution.py:661
  218.8 73.5 %shard_map.81 = (f32[32,512]{1,0:T(8,128)}, f32[32,512]{1,0:T(8,128)}) custom-call(f32[1024,2560]{1,0:T(8,128)} %bitcast.65, bf16[2,1024,512]{2,1,0:T(8,128)(2,1)} %bitcast.63), custom_call_target="tpu_custom_call" | custom-call | tf_op jit(solution)/shard_map/pallas_call | solution.py:172
  (18 shorter events, 0.1 us)
Async XLA Ops:
  0.6 151.9 %copy-start = (bf16[512,512]{1,0:T(8,128)(2,1)S(1)}, bf16[512,512]{1,0:T(8,128)(2,1)}, u32[]{:S(2)}) copy-start(bf16[512,512]{1,0:T(8,128)(2,1)} %param.11) | copy-start | bytes 1572868
  1.6 0.8 copy-start.2
  38.7 4.3 %copy-start.5 = (bf16[2,2048,224]{1,2,0:T(8,128)(2,1)S(1)}, bf16[2,2048,224]{1,2,0:T(8,128)(2,1)}, u32[]{:S(2)}) copy-start(bf16[2,2048,224]{1,2,0:T(8,128)(2,1)} %param.9) | copy-start | bytes 5505028
  43.0 3.8 %copy-start.4 = (bf16[4,4,64,2048]{3,2,1,0:T(8,128)(2,1)S(1)}, bf16[4,4,64,2048]{3,2,1,0:T(8,128)(2,1)}, u32[]{:S(2)}) copy-start(bf16[4,4,64,2048]{3,2,1,0:T(8,128)(2,1)} %get-tuple-element.7) | copy-start | bytes 12582916
  43.0 4.0 %copy-start.6 = (bf16[2,2048,224]{1,2,0:T(8,128)(2,1)S(1)}, bf16[2,2048,224]{1,2,0:T(8,128)(2,1)}, u32[]{:S(2)}) copy-start(bf16[2,2048,224]{1,2,0:T(8,128)(2,1)} %param.8) | copy-start | bytes 5505028
  47.0 2.2 copy-start.3
  52.1 58.5 %slice-start = ((s8[7340032]{0:T(1024)(128)(4,1)}), s8[4194304]{0:T(1024)(128)(4,1)S(1)}, s32[]{:S(2)}) async-start(s8[7340032]{0:T(1024)(128)(4,1)} %bitcast.78), calls=%async_computation | async-start | bytes 8388608
  52.3 58.3 %slice-start.1 = ((s8[7340032]{0:T(1024)(128)(4,1)}), s8[3145728]{0:T(1024)(128)(4,1)S(1)}, s32[]{:S(2)}) async-start(s8[7340032]{0:T(1024)(128)(4,1)} %bitcast.78), calls=%async_computation.1 | async-start | bytes 6291456
  152.5 1.3 copy-start.1

commit v5 on v4

--- a/solution.py
+++ b/solution.py
@@ -180,7 +180,7 @@
             pltpu.VMEM((tokens, rank), jnp.bfloat16),
             pltpu.VMEM((tokens, rank), jnp.bfloat16),
         ],
-        compiler_params=pltpu.CompilerParams(vmem_limit_bytes=56 * 2**20),
+        compiler_params=pltpu.CompilerParams(vmem_limit_bytes=36 * 2**20),
     )(full, acts)
 
 
@@ -320,7 +320,7 @@
     send.finish()
 
 
-def remote_call(kernel, out_shape, copies, number, scratch=(), limit=48):
+def remote_call(kernel, out_shape, copies, number, limit, scratch=()):
     return pl.pallas_call(
         kernel,
         out_shape=out_shape,
@@ -339,7 +339,51 @@
 def gather_tokens(tokens):
     rows, features = tokens.shape
     out = jax.ShapeDtypeStruct((4, 4, 4 * rows, features), tokens.dtype)
-    return remote_call(tokens_kernel, out, 19, 0)(tokens)
+    return remote_call(tokens_kernel, out, 19, 0, 12)(tokens)
+
+
+def project_kernel(x_ref, gain_ref, gate_ref, up_ref, part, squares):
+    def dot(a, b):
+        return lax.dot_general(a, b, (((1,), (1,)), ((), ())), preferred_element_type=jnp.float32)
+
+    features = x_ref.shape[1]
+    units = gate_ref.shape[1]
+    values = x_ref[...].astype(jnp.float32)
+    high, low = split(values * values)
+    ones = jnp.ones((8, features), jnp.bfloat16)
+    squares[...] = dot(ones, high) + dot(ones, low)
+    lanes = pl.ds(pl.multiple_of(lax.axis_index("dp") * features, 128), features)
+    for c in range(2):
+        scaled = (values * gain_ref[c : c + 1, lanes]).astype(jnp.bfloat16)
+        row = 2 * c * units
+        part[pl.ds(row, units), :] = dot(gate_ref[c], scaled).astype(jnp.bfloat16)
+        part[pl.ds(row + units, units), :] = dot(up_ref[c], scaled).astype(jnp.bfloat16)
+
+
+def project(tokens, norm_gain, gate_weight, up_weight):
+    count, features = tokens.shape
+    units = gate_weight.shape[2]
+    step = 256
+    whole = pl.BlockSpec((2, units, features), lambda i: (0, 0, 0))
+    return pl.pallas_call(
+        project_kernel,
+        grid=(count // step,),
+        out_shape=(
+            jax.ShapeDtypeStruct((4 * units, count), jnp.bfloat16),
+            jax.ShapeDtypeStruct((8, count), jnp.float32),
+        ),
+        in_specs=[
+            pl.BlockSpec((step, features), lambda i: (i, 0)),
+            pl.BlockSpec(norm_gain.shape, lambda i: (0, 0)),
+            whole,
+            whole,
+        ],
+        out_specs=(
+            pl.BlockSpec((4 * units, step), lambda i: (0, i)),
+            pl.BlockSpec((8, step), lambda i: (0, i)),
+        ),
+        compiler_params=pltpu.CompilerParams(vmem_limit_bytes=40 * 2**20),
+    )(tokens, norm_gain, gate_weight.swapaxes(1, 2), up_weight.swapaxes(1, 2))
 
 
 def hidden_kernel(part, squares, out, near, near_sq, pair, pair_sq, far, far_sq, send_sem, recv_sem):
@@ -486,7 +530,7 @@
         pltpu.VMEM((2, rows, tokens // 2), jnp.bfloat16),
         pltpu.VMEM((8, tokens), jnp.float32),
     ]
-    return remote_call(hidden_kernel, out, 41, 1, scratch)(part, squares)
+    return remote_call(hidden_kernel, out, 41, 1, 24, scratch)(part, squares)
 
 
 def acts_kernel(part, out, landed, send_sem, recv_sem):
@@ -502,43 +546,52 @@
     sibling = {"dp": zh * 2 + 1 - core}
     greet(mates + [right, left, sibling])
     send = Sender(send_sem, recv_sem)
-    sums = [send(part.at[(m + k) % 4], landed.at[k - 1], mates[k - 1]) for k in range(1, 4)]
-    for copy in sums:
-        copy.wait_recv()
-
+    sums = [
+        [
+            send(part.at[(m + k) % 4, c], landed.at[k - 1, c], mates[k - 1])
+            for k in (2, 1, 3)
+        ]
+        for c in range(2)
+    ]
+    half = part.shape[2] // 2
+    halves = pl.ds(0, half), pl.ds(half, half)
+
+    def block(c, chip):
+        return out.at[c, core * 8 + chip]
+
+    shared = []
+    waiting = []
     for c in range(2):
+        for copy in sums[c]:
+            copy.wait_recv()
         total = part[m, c].astype(jnp.float32)
         for k in range(3):
             total += landed[k, c].astype(jnp.float32)
         out[c, core * 8 + z] = total.astype(jnp.bfloat16)
-
-    def block(chip):
-        return out.at[:, core * 8 + chip]
-
-    from_left = send(block(z), block(z), right)
-    from_right = send(block(z), block(z), left)
-    shared = [send(block(z), block(z), sibling)]
+        here = block(c, z)
+        waiting.append((send(here, here, right), send(here, here, left)))
+        shared.append(send(here, here, sibling))
     for k in range(1, 4):
         before, after = (z + 8 - k) % 8, (z + k) % 8
-        from_left.wait_recv()
-        if k < 3:
-            next_left = send(block(before), block(before), right)
-        else:
-            piece = out.at[0, core * 8 + before]
-            next_left = send(piece, piece, right)
-        from_right.wait_recv()
-        if k < 3:
-            next_right = send(block(after), block(after), left)
-        else:
-            piece = out.at[1, core * 8 + after]
-            next_right = send(piece, piece, left)
-        shared.append(send(block(before), block(before), sibling))
-        shared.append(send(block(after), block(after), sibling))
-        from_left, from_right = next_left, next_right
-    from_left.wait_recv()
-    from_right.wait_recv()
+        for c in range(2):
+            from_left, from_right = waiting[c]
+            near, next_near = block(c, before), block(c, after)
+            on, back = near, next_near
+            if k == 3:
+                on = out.at[c, core * 8 + before, halves[0]]
+                back = out.at[c, core * 8 + after, halves[1]]
+            from_left.wait_recv()
+            next_left = send(on, on, right)
+            from_right.wait_recv()
+            next_right = send(back, back, left)
+            shared.append(send(near, near, sibling))
+            shared.append(send(next_near, next_near, sibling))
+            waiting[c] = (next_left, next_right)
     far = (z + 4) % 8
-    shared.append(send(block(far), block(far), sibling))
+    for c in range(2):
+        for copy in waiting[c]:
+            copy.wait_recv()
+        shared.append(send(block(c, far), block(c, far), sibling))
     for copy in shared:
         copy.wait_recv()
     send.finish()
@@ -548,7 +601,7 @@
     _, copies, rows, features = part.shape
     out = jax.ShapeDtypeStruct((copies, 16, rows, features), jnp.bfloat16)
     scratch = [pltpu.VMEM((3, copies, rows, features), jnp.bfloat16)]
-    return remote_call(acts_kernel, out, 19, 2, scratch)(part)
+    return remote_call(acts_kernel, out, 38, 2, 12, scratch)(part)
 
 
 def rows_kernel(part, out, landed, send_sem, recv_sem):
@@ -658,7 +711,7 @@
     rows, width = part.shape
     out = jax.ShapeDtypeStruct((16, 4, 2, rows // 8, width), jnp.float32)
     scratch = [pltpu.VMEM((15, rows // 8, width // 2), jnp.float32)]
-    full = remote_call(rows_kernel, out, 46, 3, scratch)(part.reshape(4, 2, rows // 8, width))
+    full = remote_call(rows_kernel, out, 46, 3, 24, scratch)(part.reshape(4, 2, rows // 8, width))
     return full.reshape(16 * rows, width)
 
 
@@ -668,18 +721,9 @@
 
 def on_device(tokens, norm_gain, gate_weight, up_weight, down_weight, sketch):
     feature_count = tokens.shape[1]
-    offset = lax.axis_index("dp") * feature_count
-    local_gain = lax.dynamic_slice_in_dim(norm_gain, offset, feature_count, 1)
     gathered = gather_tokens(tokens).reshape(-1, feature_count)
     count = gathered.shape[0]
-    values = gathered.astype(jnp.float32)
-    squares = jnp.broadcast_to(jnp.sum(values * values, axis=1), (8, count))
-    parts = []
-    for c in range(2):
-        scaled = (values * local_gain[c]).astype(jnp.bfloat16)
-        for weight in (gate_weight[c], up_weight[c]):
-            parts.append(against(weight, scaled, ((0,), (1,))).astype(jnp.bfloat16))
-    part = jnp.concatenate(parts, axis=0)
+    part, squares = project(gathered, norm_gain, gate_weight, up_weight)
     hidden = sum_and_gather_hidden(part, squares)
     hidden = hidden.reshape(2, -1, hidden.shape[-1])
     partial_out = jnp.stack(

time: 292 us -> 273 us (0.935)
  matrix products: 11.4 us -> 3.33 us
  Pallas kernels: 272 us -> 267 us
  other arithmetic: 4.42 us -> 0.1 us
    dot_general x9 -> x5, matrix products: 11.4 us -> 3.33 us  [against(): lax.dot_general(left, right, (dims, ((), ())), preferred_element_type=jnp...]
    pallas_call x1, Pallas kernels: 73.5 us -> 68.9 us  [sketch_call(): pl.pallas_call(sketch_kernel, out_shape=(shape, shape), in_specs=[pl.Bloc...]
    reduce_sum x1 -> x0, other arithmetic: 4.18 us -> none  [on_device(): squares = jnp.broadcast_to(jnp.sum(values * values, axis=1), (8, count))]
    pallas_call x4 -> x5, Pallas kernels: 199 us -> 198 us  [the longest x1 60 us: sum_and_gather_rows(): remote_call(rows_kernel, out, 46, 3, 24, scratch)]
where the time goes in v5:
time: 273 us
  Pallas kernels  267 us (98%)
  matrix products  3.33 us (1%)
    pallas_call x1, Pallas kernels, sketch_call(): pl.pallas_call(sketch_kernel, out_shape=(shape, shape), in_specs=[pl.Bloc...  68.9 us
    pallas_call x1, Pallas kernels, sum_and_gather_rows(): remote_call(rows_kernel, out, 46, 3, 24, scratch)  60 us
    pallas_call x1, Pallas kernels, sum_and_gather_hidden(): return remote_call(hidden_kernel, out, 41, 1, 24, scratch)(part, squares)  57.8 us
    pallas_call x1, Pallas kernels, sum_and_gather_acts(): return remote_call(acts_kernel, out, 38, 2, 12, scratch)(part)  36.6 us
    pallas_call x1, Pallas kernels, gather_tokens(): return remote_call(tokens_kernel, out, 19, 0, 12)(tokens)  36.3 us
    pallas_call x1, Pallas kernels, project(): pl.pallas_call(project_kernel, grid=(count // step,), out_shape=(jax.Shap...  7.72 us

profile of v5, /device:TPU:1, one launch (start us, length us, event | category | flops | bytes accessed | tf_op | source)
XLA Modules:
  0.0 272.9 jit_solution(17459285886688450881)
XLA Ops:
  0.6 0.0 copy-start
  0.7 0.0 copy-start.3
  0.7 0.9 copy-done.3
  1.6 36.3 %shard_map.77 = bf16[4,4,64,2048]{3,2,1,0:T(8,128)(2,1)S(1)} custom-call(bf16[16,2048]{1,0:T(8,128)(2,1)S(1)} %copy-done.3), custom_call_target="tpu_custom_call" | custom-call | tf_op jit(solution)/shard_map/pallas_call | solution.py:342
  37.9 0.0 copy-done.1
  37.9 0.0 copy-done.2
  37.9 0.0 copy-done.4
  37.9 0.0 slice-start
  37.9 7.7 %shard_map.78 = (bf16[896,1024]{1,0:T(8,128)(2,1)S(1)}, f32[8,1024]{1,0:T(8,128)S(1)}) custom-call(bf16[1024,2048]{1,0:T(8,128)(2,1)S(1)} %bitcast.40, f32[2,8192]{1,0:T(2,128)S(1)} %copy-done.4, bf16[2,224,2048]{2,1,0:T(8,128)(2,1)S(1)} %bitcast.42, bf16[2,224,2048]{2,1,0:T(8,128)(2,1)S(1)} %bitcast.43), custom_call_target="tpu_custom_call" | custom-call | tf_op jit(solution)/shard_map/pallas_call | solution.py:368
  45.6 0.0 slice-start.1
  45.6 57.8 %shard_map.79 = bf16[2,4,4,224,256]{4,3,2,1,0:T(8,128)(2,1)S(1)} custom-call(bf16[896,1024]{1,0:T(8,128)(2,1)S(1)} %get-tuple-element.6.part, f32[8,1024]{1,0:T(8,128)S(1)} %get-tuple-element.7.squares), custom_call_target="tpu_custom_call" | custom-call | tf_op jit(solution)/shard_map/pallas_call | solution.py:533
  103.4 0.2 fusion.18
  103.7 0.0 slice-done
  103.7 1.1 fusion.6
  104.8 1.1 fusion.9
  106.0 0.1 maximum_bitcast_fusion.part
  106.0 36.6 %shard_map.80 = bf16[2,16,64,512]{3,2,1,0:T(8,128)(2,1)S(1)} custom-call(bf16[4,2,64,512]{3,2,1,0:T(8,128)(2,1)S(1)} %maximum_bitcast_fusion.part), custom_call_target="tpu_custom_call" | custom-call | tf_op jit(solution)/shard_map/pallas_call | solution.py:604
  142.6 0.2 fusion.13
  142.8 0.2 fusion.19
  143.1 0.4 fusion.12
  143.5 0.4 fusion.14
  143.9 0.1 pad_maximum_fusion
  144.0 60.0 %shard_map.81 = f32[16,4,2,8,2560]{4,3,2,1,0:T(8,128)S(1)} custom-call(f32[4,2,8,2560]{3,2,1,0:T(8,128)S(1)} %bitcast.41), custom_call_target="tpu_custom_call" | custom-call | tf_op jit(solution)/shard_map/pallas_call | solution.py:714
  203.9 68.9 %shard_map.82 = (f32[32,512]{1,0:T(8,128)}, f32[32,512]{1,0:T(8,128)}) custom-call(f32[1024,2560]{1,0:T(8,128)S(1)} %bitcast.38, bf16[2,1024,512]{2,1,0:T(8,128)(2,1)S(1)} %bitcast.39), custom_call_target="tpu_custom_call" | custom-call | tf_op jit(solution)/shard_map/pallas_call | solution.py:172
  (6 shorter events, 0.0 us)
Async XLA Ops:
  0.6 142.0 %copy-start = (bf16[512,512]{1,0:T(8,128)(2,1)S(1)}, bf16[512,512]{1,0:T(8,128)(2,1)}, u32[]{:S(2)}) copy-start(bf16[512,512]{1,0:T(8,128)(2,1)} %param.11) | copy-start | bytes 1572868
  0.7 0.9 copy-start.3
  1.6 36.3 %copy-start.1 = (bf16[2,2048,224]{1,2,0:T(8,128)(2,1)S(1)}, bf16[2,2048,224]{1,2,0:T(8,128)(2,1)}, u32[]{:S(2)}) copy-start(bf16[2,2048,224]{1,2,0:T(8,128)(2,1)} %param.8) | copy-start | bytes 5505028
  1.6 36.3 %copy-start.2 = (bf16[2,2048,224]{1,2,0:T(8,128)(2,1)S(1)}, bf16[2,2048,224]{1,2,0:T(8,128)(2,1)}, u32[]{:S(2)}) copy-start(bf16[2,2048,224]{1,2,0:T(8,128)(2,1)} %param.9) | copy-start | bytes 5505028
  1.6 36.3 %copy-start.4 = (f32[2,8192]{1,0:T(2,128)S(1)}, f32[2,8192]{1,0:T(2,128)}, u32[]{:S(2)}) copy-start(f32[2,8192]{1,0:T(2,128)} %gain_ref.1) | copy-start | bytes 196612
  37.9 65.8 %slice-start = ((s8[7340032]{0:T(1024)(128)(4,1)}), s8[4194304]{0:T(1024)(128)(4,1)S(1)}, s32[]{:S(2)}) async-start(s8[7340032]{0:T(1024)(128)(4,1)} %bitcast.50), calls=%async_computation | async-start | bytes 8388608
  45.6 58.1 %slice-start.1 = ((s8[7340032]{0:T(1024)(128)(4,1)}), s8[3145728]{0:T(1024)(128)(4,1)S(1)}, s32[]{:S(2)}) async-start(s8[7340032]{0:T(1024)(128)(4,1)} %bitcast.50), calls=%async_computation.1 | async-start | bytes 6291456

commit v6 on v5

--- a/solution.py
+++ b/solution.py
@@ -10,6 +10,7 @@
 D = 8192
 EPSILON = 1e-05
 BLOCK = 128
+HALF = 4
 
 
 def split(value):
@@ -125,18 +126,31 @@
             inv = following
 
 
-def sketch_kernel(full, acts, basis_out, last_out, gram, low_inv, high_z, low_z):
+def fill_grams(full, g_high, g_low):
+    @pl.loop(0, 2 * HALF)
+    def _(z):
+        here = pl.ds(pl.multiple_of(z * BLOCK, BLOCK), BLOCK)
+        for c in range(2):
+            for k in range(HALF + 1):
+                there = pl.ds(pl.multiple_of(((z + k) % 8) * BLOCK, BLOCK), BLOCK)
+                value = full[here, pl.ds((c * (HALF + 1) + k) * BLOCK, BLOCK)]
+                g_high[c, here, there], g_low[c, here, there] = split(value)
+                if 0 < k < HALF:
+                    g_high[c, there, here], g_low[c, there, here] = split(value.T)
+
+
+def sketch_kernel(full, acts, basis_out, last_out, gram, low_inv, high_z, low_z, g_high, g_low):
     tokens = full.shape[0]
     rank = gram.shape[0]
     share = basis_out.shape[0]
-    high, low = split(full[:, pl.ds(2 * tokens, rank)])
+    high, low = split(full[:, pl.ds(2 * (HALF + 1) * BLOCK, rank)])
     high_z[...] = high
     low_z[...] = low
+    fill_grams(full, g_high, g_low)
 
     def step(n, carry):
-        g_s = split(full[:, pl.ds(pl.multiple_of((n % 2) * tokens, 128), tokens)])
         z_s = (high_z[...], low_z[...])
-        h = mul(g_s, z_s)
+        h = mul((g_high[n % 2], g_low[n % 2]), z_s)
         gram[...] = mul(z_s, split(h), ((0,), (0,))) * (2.0**-33)
         orth_factor(gram, low_inv)
 
@@ -152,7 +166,7 @@
     index = lax.axis_index("mp") * 4 + lax.axis_index("dp")
     rows = low_inv[pl.ds(pl.multiple_of(index * share, share), share), :]
     coeff = split(mul(split(rows), (high_z[...], low_z[...]), ((1,), (1,))) * (1.0 / 1024))
-    last = split(mul(coeff, split(full[:, pl.ds(0, tokens)])) * (1.0 / 1024))
+    last = split(mul(coeff, (g_high[0], g_low[0])) * (1.0 / 1024))
 
     def apply(pair, c):
         def dot(a):
@@ -166,7 +180,7 @@
 
 def sketch_call(full, acts):
     tokens = full.shape[0]
-    rank = full.shape[1] - 2 * tokens
+    rank = full.shape[1] - 2 * (HALF + 1) * BLOCK
     features = acts.shape[2]
     shape = jax.ShapeDtypeStruct((rank // 16, features), jnp.float32)
     return pl.pallas_call(
@@ -179,6 +193,8 @@
             pltpu.VMEM((rank, rank), jnp.float32),
             pltpu.VMEM((tokens, rank), jnp.bfloat16),
             pltpu.VMEM((tokens, rank), jnp.bfloat16),
+            pltpu.VMEM((2, tokens, tokens), jnp.bfloat16),
+            pltpu.VMEM((2, tokens, tokens), jnp.bfloat16),
         ],
         compiler_params=pltpu.CompilerParams(vmem_limit_bytes=36 * 2**20),
     )(full, acts)
@@ -557,7 +573,7 @@
     halves = pl.ds(0, half), pl.ds(half, half)
 
     def block(c, chip):
-        return out.at[c, core * 8 + chip]
+        return out.at[c, chip * 2 + core]
 
     shared = []
     waiting = []
@@ -567,7 +583,7 @@
         total = part[m, c].astype(jnp.float32)
         for k in range(3):
             total += landed[k, c].astype(jnp.float32)
-        out[c, core * 8 + z] = total.astype(jnp.bfloat16)
+        out[c, z * 2 + core] = total.astype(jnp.bfloat16)
         here = block(c, z)
         waiting.append((send(here, here, right), send(here, here, left)))
         shared.append(send(here, here, sibling))
@@ -578,8 +594,8 @@
             near, next_near = block(c, before), block(c, after)
             on, back = near, next_near
             if k == 3:
-                on = out.at[c, core * 8 + before, halves[0]]
-                back = out.at[c, core * 8 + after, halves[1]]
+                on = out.at[c, before * 2 + core, halves[0]]
+                back = out.at[c, after * 2 + core, halves[1]]
             from_left.wait_recv()
             next_left = send(on, on, right)
             from_right.wait_recv()
@@ -633,20 +649,19 @@
     for k in range(15):
         sums[k].wait_recv()
         total += landed[k]
-    mine = core * 8 + z
-    out[mine, x, y // 2, :, column(y)] = total
-    own = out.at[mine, x, y // 2, :, column(y)]
+    out[z, core, x, y // 2, :, column(y)] = total
+    own = out.at[z, core, x, y // 2, :, column(y)]
     spread = [send(own, own, chip) for chip in chips]
     for copy in spread:
         copy.wait_recv()
 
-    low, high = pl.ds(core * 8, 4), pl.ds(core * 8 + 4, 4)
-    low_a, low_b = pl.ds(core * 8, 2), pl.ds(core * 8 + 2, 2)
-    high_a, high_b = pl.ds(core * 8 + 4, 2), pl.ds(core * 8 + 6, 2)
+    low, high = pl.ds(0, 4), pl.ds(4, 4)
+    low_a, low_b = pl.ds(0, 2), pl.ds(2, 2)
+    high_a, high_b = pl.ds(4, 2), pl.ds(6, 2)
     two, rest = pl.ds(0, 2), pl.ds(2, 2)
 
     def cell(members, i, j):
-        return out.at[members, i, j // 2, :, column(j)]
+        return out.at[members, core, i, j // 2, :, column(j)]
 
     def piece_a(phase):
         if phase == 0:
@@ -675,9 +690,9 @@
                 along_y(x),
             )
         return (
-            lambda i: out.at[high, i],
-            lambda i: out.at[high_a, i],
-            lambda i: out.at[high_b, i],
+            lambda i: out.at[high, core, i],
+            lambda i: out.at[high_a, core, i],
+            lambda i: out.at[high_b, core, i],
             x,
             along_x(y),
         )
@@ -709,10 +724,39 @@
 
 def sum_and_gather_rows(part):
     rows, width = part.shape
-    out = jax.ShapeDtypeStruct((16, 4, 2, rows // 8, width), jnp.float32)
+    out = jax.ShapeDtypeStruct((8, 2, 4, 2, rows // 8, width), jnp.float32)
     scratch = [pltpu.VMEM((15, rows // 8, width // 2), jnp.float32)]
     full = remote_call(rows_kernel, out, 46, 3, 24, scratch)(part.reshape(4, 2, rows // 8, width))
     return full.reshape(16 * rows, width)
+
+
+def products_kernel(acts, sketch, out):
+    d = lax.axis_index("dp")
+    core = d % 2
+    z = (d // 2) * 4 + lax.axis_index("mp")
+    rows = out.shape[0]
+    for c in range(2):
+        mine = acts[c, z, pl.ds(pl.multiple_of(core * rows, rows), rows)]
+        for k in range(HALF + 1):
+            other = acts[c, lax.rem(z + k, 8)]
+            lanes = pl.ds((c * (HALF + 1) + k) * BLOCK, BLOCK)
+            out[:, lanes] = lax.dot_general(
+                mine, other, (((1,), (1,)), ((), ())), preferred_element_type=jnp.float32
+            )
+    lanes = pl.ds(2 * (HALF + 1) * BLOCK, sketch.shape[1])
+    out[:, lanes] = jnp.dot(mine, sketch[...], preferred_element_type=jnp.float32)
+
+
+def row_products(acts, sketch):
+    rows = acts.shape[2] // 2
+    width = 2 * (HALF + 1) * BLOCK + sketch.shape[1]
+    return pl.pallas_call(
+        products_kernel,
+        out_shape=jax.ShapeDtypeStruct((rows, width), jnp.float32),
+        in_specs=[VMEM, VMEM],
+        out_specs=VMEM,
+        compiler_params=pltpu.CompilerParams(vmem_limit_bytes=12 * 2**20),
+    )(acts, sketch)
 
 
 def against(left, right, dims):
@@ -737,17 +781,7 @@
     partial_out = partial_out.reshape(share_mp, -1, 2, partial_out.shape[-1]).swapaxes(1, 2)
     blocks = sum_and_gather_acts(partial_out)
     acts = blocks.reshape(2, count, -1)
-    d = lax.axis_index("dp")
-    index = (d % 2) * 8 + (d // 2) * 4 + lax.axis_index("mp")
-    mine = lax.dynamic_index_in_dim(blocks, index, 1, keepdims=False)
-    rows = jnp.concatenate(
-        [
-            against(mine[0], acts[0], ((1,), (1,))),
-            against(mine[1], acts[1], ((1,), (1,))),
-            against(mine[1], sketch, ((1,), (0,))),
-        ],
-        axis=1,
-    )
+    rows = row_products(blocks.reshape(2, 8, count // 8, -1), sketch)
     full = sum_and_gather_rows(rows)
     basis_share, projected = sketch_call(full, acts)
     return (basis_share.T, projected.T)

time: 273 us -> 263 us (0.963)
  Pallas kernels: 267 us -> 258 us
    pallas_call x1, Pallas kernels: 60 us -> 48 us  [sum_and_gather_rows(): remote_call(rows_kernel, out, 46, 3, 24, scratch)]
where the time goes in v6:
time: 263 us
  Pallas kernels  258 us (98%)
    pallas_call x1, Pallas kernels, sketch_call(): pl.pallas_call(sketch_kernel, out_shape=(shape, shape), in_specs=[pl.Bloc...  71.4 us
    pallas_call x1, Pallas kernels, sum_and_gather_hidden(): return remote_call(hidden_kernel, out, 41, 1, 24, scratch)(part, squares)  57.2 us
    pallas_call x1, Pallas kernels, sum_and_gather_rows(): remote_call(rows_kernel, out, 46, 3, 24, scratch)  48 us
    pallas_call x1, Pallas kernels, sum_and_gather_acts(): return remote_call(acts_kernel, out, 38, 2, 12, scratch)(part)  37.1 us
    pallas_call x1, Pallas kernels, gather_tokens(): return remote_call(tokens_kernel, out, 19, 0, 12)(tokens)  36.3 us
    pallas_call x1, Pallas kernels, project(): pl.pallas_call(project_kernel, grid=(count // step,), out_shape=(jax.Shap...  7.72 us

profile of v6, /device:TPU:1, one launch (start us, length us, event | category | flops | bytes accessed | tf_op | source)
XLA Modules:
  0.0 262.6 jit_solution(3183457247081655381)
XLA Ops:
  0.6 0.0 copy-start.3
  0.6 0.8 copy-done.3
  1.5 0.0 copy-start
  1.5 0.0 copy-start.1
  1.5 36.3 %shard_map.77 = bf16[4,4,64,2048]{3,2,1,0:T(8,128)(2,1)S(1)} custom-call(bf16[16,2048]{1,0:T(8,128)(2,1)S(1)} %copy-done.3), custom_call_target="tpu_custom_call" | custom-call | tf_op jit(solution)/shard_map/pallas_call | solution.py:358
  37.8 0.0 copy-done
  37.8 0.0 copy-done.1
  37.8 0.0 copy-done.4
  37.8 0.0 slice-start
  37.8 7.7 %shard_map.78 = (bf16[896,1024]{1,0:T(8,128)(2,1)S(1)}, f32[8,1024]{1,0:T(8,128)S(1)}) custom-call(bf16[1024,2048]{1,0:T(8,128)(2,1)S(1)} %bitcast.30, f32[2,8192]{1,0:T(2,128)S(1)} %copy-done.4, bf16[2,224,2048]{2,1,0:T(8,128)(2,1)S(1)} %bitcast.31, bf16[2,224,2048]{2,1,0:T(8,128)(2,1)S(1)} %bitcast.32), custom_call_target="tpu_custom_call" | custom-call | tf_op jit(solution)/shard_map/pallas_call | solution.py:384
  45.5 0.0 slice-start.1
  45.5 57.2 %shard_map.79 = bf16[2,4,4,224,256]{4,3,2,1,0:T(8,128)(2,1)S(1)} custom-call(bf16[896,1024]{1,0:T(8,128)(2,1)S(1)} %get-tuple-element.6.part, f32[8,1024]{1,0:T(8,128)S(1)} %get-tuple-element.7.squares), custom_call_target="tpu_custom_call" | custom-call | tf_op jit(solution)/shard_map/pallas_call | solution.py:549
  102.8 0.2 fusion.12
  103.0 0.0 slice-done
  103.1 0.0 slice-done.1
  103.1 1.1 fusion.6
  104.2 1.1 fusion.9
  105.3 0.0 copy-start.2
  105.4 0.1 maximum_bitcast_fusion.part
  105.4 37.1 %shard_map.80 = bf16[2,16,64,512]{3,2,1,0:T(8,128)(2,1)S(1)} custom-call(bf16[4,2,64,512]{3,2,1,0:T(8,128)(2,1)S(1)} %maximum_bitcast_fusion.part), custom_call_target="tpu_custom_call" | custom-call | tf_op jit(solution)/shard_map/pallas_call | solution.py:620
  142.5 0.0 copy-done.2
  142.5 0.7 shard_map.81
  143.2 48.0 %shard_map.82 = f32[8,2,4,2,8,1792]{5,4,3,2,1,0:T(8,128)S(1)} custom-call(f32[4,2,8,1792]{3,2,1,0:T(8,128)S(1)} %bitcast.33), custom_call_target="tpu_custom_call" | custom-call | tf_op jit(solution)/shard_map/pallas_call | solution.py:729
  191.3 71.4 %shard_map.83 = (f32[32,512]{1,0:T(8,128)}, f32[32,512]{1,0:T(8,128)}) custom-call(f32[1024,1792]{1,0:T(8,128)S(1)} %bitcast.27, bf16[2,1024,512]{2,1,0:T(8,128)(2,1)S(1)} %bitcast.29), custom_call_target="tpu_custom_call" | custom-call | tf_op jit(solution)/shard_map/pallas_call | solution.py:186
  (2 shorter events, 0.0 us)
Async XLA Ops:
  0.6 0.8 copy-start.3
  1.5 36.3 %copy-start = (bf16[2,2048,224]{1,2,0:T(8,128)(2,1)S(1)}, bf16[2,2048,224]{1,2,0:T(8,128)(2,1)}, u32[]{:S(2)}) copy-start(bf16[2,2048,224]{1,2,0:T(8,128)(2,1)} %param.8) | copy-start | bytes 5505028
  1.5 36.3 %copy-start.1 = (bf16[2,2048,224]{1,2,0:T(8,128)(2,1)S(1)}, bf16[2,2048,224]{1,2,0:T(8,128)(2,1)}, u32[]{:S(2)}) copy-start(bf16[2,2048,224]{1,2,0:T(8,128)(2,1)} %param.9) | copy-start | bytes 5505028
  1.5 36.3 %copy-start.4 = (f32[2,8192]{1,0:T(2,128)S(1)}, f32[2,8192]{1,0:T(2,128)}, u32[]{:S(2)}) copy-start(f32[2,8192]{1,0:T(2,128)} %gain_ref.1) | copy-start | bytes 196612
  37.8 65.3 %slice-start = ((s8[7340032]{0:T(1024)(128)(4,1)}), s8[3145728]{0:T(1024)(128)(4,1)S(1)}, s32[]{:S(2)}) async-start(s8[7340032]{0:T(1024)(128)(4,1)} %bitcast.38), calls=%async_computation | async-start | bytes 6291456
  45.5 57.5 %slice-start.1 = ((s8[7340032]{0:T(1024)(128)(4,1)}), s8[4194304]{0:T(1024)(128)(4,1)S(1)}, s32[]{:S(2)}) async-start(s8[7340032]{0:T(1024)(128)(4,1)} %bitcast.38), calls=%async_computation.1 | async-start | bytes 8388608
  105.3 37.2 %copy-start.2 = (bf16[512,512]{1,0:T(8,128)(2,1)S(1)}, bf16[512,512]{1,0:T(8,128)(2,1)}, u32[]{:S(2)}) copy-start(bf16[512,512]{1,0:T(8,128)(2,1)} %sketch.1) | copy-start | bytes 1572868

commit v7 on v6

--- a/solution.py
+++ b/solution.py
@@ -254,13 +254,29 @@
     return forward
 
 
-def two_rings(send, piece_a, piece_b):
-    for phase in range(2):
-        a = ring(send, *piece_a(phase))
-        b = ring(send, *piece_b(phase))
-        pending = [*a(), *b()]
-        for copy in pending:
-            copy.wait_recv()
+def crossed_rings(send, plans, middle=None):
+    def along_first(plan):
+        cell, me, toward, me_next, _ = plan
+        return ring(send, *(lambda i, p=p: cell(i, me_next, p) for p in range(3)), me, toward)
+
+    def along_second(plan, shift):
+        cell, me, _, me_next, toward_next = plan
+        i = (me + shift) % 4
+        return ring(send, *(lambda j, p=p: cell(i, j, p) for p in range(3)), me_next, toward_next)
+
+    first = [along_first(plan) for plan in plans]
+    own = [along_second(plan, 0) for plan in plans]
+    last = [copy for forward in first for copy in forward()]
+    sides = [along_second(plan, shift) for shift in (3, 1) for plan in plans]
+    pending = [copy for forward in own for copy in forward()]
+    for copy in last:
+        copy.wait_recv()
+    opposite = [along_second(plan, 2) for plan in plans]
+    if middle is not None:
+        middle()
+    for forward in sides + opposite:
+        pending += forward()
+    return pending
 
 
 def along_x(y):
@@ -296,43 +312,11 @@
     count = 4 * rows
     a, b = pl.ds(0, half), pl.ds(half, half)
     up, down = pl.ds(0, count // 2), pl.ds(count // 2, count // 2)
-    two, rest = pl.ds(0, 2), pl.ds(2, 2)
-
-    def piece_a(phase):
-        if phase == 0:
-            return (
-                lambda i: out.at[i, y, :, a],
-                lambda i: out.at[i, y, up, a],
-                lambda i: out.at[i, y, down, a],
-                x,
-                along_x(y),
-            )
-        return (
-            lambda i: out.at[:, i, :, a],
-            lambda i: out.at[two, i, :, a],
-            lambda i: out.at[rest, i, :, a],
-            y,
-            along_y(x),
-        )
-
-    def piece_b(phase):
-        if phase == 0:
-            return (
-                lambda i: out.at[x, i, :, b],
-                lambda i: out.at[x, i, up, b],
-                lambda i: out.at[x, i, down, b],
-                y,
-                along_y(x),
-            )
-        return (
-            lambda i: out.at[i, :, :, b],
-            lambda i: out.at[i, two, :, b],
-            lambda i: out.at[i, rest, :, b],
-            x,
-            along_x(y),
-        )
-
-    two_rings(send, piece_a, piece_b)
+    part = slice(None), up, down
+    plan_a = (lambda i, j, p: out.at[i, j, part[p], a], x, along_x(y), y, along_y(x))
+    plan_b = (lambda i, j, p: out.at[j, i, part[p], b], y, along_y(x), x, along_x(y))
+    for copy in crossed_rings(send, (plan_a, plan_b)):
+        copy.wait_recv()
     send.finish()
 
 
@@ -355,7 +339,7 @@
 def gather_tokens(tokens):
     rows, features = tokens.shape
     out = jax.ShapeDtypeStruct((4, 4, 4 * rows, features), tokens.dtype)
-    return remote_call(tokens_kernel, out, 19, 0, 12)(tokens)
+    return remote_call(tokens_kernel, out, 43, 0, 12)(tokens)
 
 
 def project_kernel(x_ref, gain_ref, gate_ref, up_ref, part, squares):
@@ -655,68 +639,28 @@
     for copy in spread:
         copy.wait_recv()
 
-    low, high = pl.ds(0, 4), pl.ds(4, 4)
-    low_a, low_b = pl.ds(0, 2), pl.ds(2, 2)
-    high_a, high_b = pl.ds(4, 2), pl.ds(6, 2)
-    two, rest = pl.ds(0, 2), pl.ds(2, 2)
+    low = pl.ds(0, 4), pl.ds(0, 2), pl.ds(2, 2)
+    high = pl.ds(4, 4), pl.ds(4, 2), pl.ds(6, 2)
 
     def cell(members, i, j):
         return out.at[members, core, i, j // 2, :, column(j)]
 
-    def piece_a(phase):
-        if phase == 0:
-            return (
-                lambda i: cell(low, i, y),
-                lambda i: cell(low_a, i, y),
-                lambda i: cell(low_b, i, y),
-                x,
-                along_x(y),
-            )
-        return (
-            lambda j: cell(low, slice(None), j),
-            lambda j: cell(low, two, j),
-            lambda j: cell(low, rest, j),
-            y,
-            along_y(x),
-        )
-
-    def piece_b(phase):
-        if phase == 0:
-            return (
-                lambda j: cell(high, x, j),
-                lambda j: cell(high_a, x, j),
-                lambda j: cell(high_b, x, j),
-                y,
-                along_y(x),
-            )
-        return (
-            lambda i: out.at[high, core, i],
-            lambda i: out.at[high_a, core, i],
-            lambda i: out.at[high_b, core, i],
-            x,
-            along_x(y),
-        )
-
+    plan_a = (lambda i, j, p: cell(low[p], i, j), x, along_x(y), y, along_y(x))
+    plan_b = (lambda i, j, p: cell(high[p], j, i), y, along_y(x), x, along_x(y))
     shared = []
 
-    def share(source):
-        shared.append(send(source, source, sibling))
-
-    a, b = ring(send, *piece_a(0)), ring(send, *piece_b(0))
-    for copy in [*a(), *b()]:
-        copy.wait_recv()
-    a, b = ring(send, *piece_a(1)), ring(send, *piece_b(1))
-    block_a, block_b = piece_a(1)[0], piece_b(1)[0]
-    share(block_a(y))
-    share(block_b(x))
-    pending = [*a(), *b()]
-    for side in (3, 1):
-        share(block_a((y + side) % 4))
-        share(block_b((x + side) % 4))
+    def share(shift):
+        across_a = cell(low[0], slice(None), (y + shift) % 4)
+        across_b = out.at[high[0], core, (x + shift) % 4]
+        shared.append(send(across_a, across_a, sibling))
+        shared.append(send(across_b, across_b, sibling))
+
+    pending = crossed_rings(send, (plan_a, plan_b), lambda: share(0))
+    share(3)
+    share(1)
     for copy in pending:
         copy.wait_recv()
-    share(block_a((y + 2) % 4))
-    share(block_b((x + 2) % 4))
+    share(2)
     for copy in shared:
         copy.wait_recv()
     send.finish()
@@ -726,7 +670,7 @@
     rows, width = part.shape
     out = jax.ShapeDtypeStruct((8, 2, 4, 2, rows // 8, width), jnp.float32)
     scratch = [pltpu.VMEM((15, rows // 8, width // 2), jnp.float32)]
-    full = remote_call(rows_kernel, out, 46, 3, 24, scratch)(part.reshape(4, 2, rows // 8, width))
+    full = remote_call(rows_kernel, out, 70, 3, 24, scratch)(part.reshape(4, 2, rows // 8, width))
     return full.reshape(16 * rows, width)
 
 

time: 263 us -> 253 us (0.962)
  Pallas kernels: 258 us -> 249 us
    pallas_call x1, Pallas kernels: 57.2 us -> 50.9 us  [sum_and_gather_hidden(): return remote_call(hidden_kernel, out, 41, 1, 24, scratch)(part, squares)]
    pallas_call x2, Pallas kernels: 84.3 us -> 80.1 us  [the longest x1 44.9 us: sum_and_gather_rows(): remote_call(rows_kernel, out, 70, 3, 24, scratch)]
where the time goes in v7:
time: 253 us
  Pallas kernels  249 us (98%)
    pallas_call x1, Pallas kernels, sketch_call(): pl.pallas_call(sketch_kernel, out_shape=(shape, shape), in_specs=[pl.Bloc...  71.4 us
    pallas_call x1, Pallas kernels, sum_and_gather_hidden(): return remote_call(hidden_kernel, out, 41, 1, 24, scratch)(part, squares)  50.9 us
    pallas_call x1, Pallas kernels, sum_and_gather_rows(): remote_call(rows_kernel, out, 70, 3, 24, scratch)  44.9 us
    pallas_call x1, Pallas kernels, sum_and_gather_acts(): return remote_call(acts_kernel, out, 38, 2, 12, scratch)(part)  38.1 us
    pallas_call x1, Pallas kernels, gather_tokens(): return remote_call(tokens_kernel, out, 43, 0, 12)(tokens)  35.2 us
    pallas_call x1, Pallas kernels, project(): pl.pallas_call(project_kernel, grid=(count // step,), out_shape=(jax.Shap...  7.72 us

profile of v7, /device:TPU:1, one launch (start us, length us, event | category | flops | bytes accessed | tf_op | source)
XLA Modules:
  0.0 253.1 jit_solution(13655685732986034482)
XLA Ops:
  0.6 0.0 copy-start.3
  0.6 0.8 copy-done.3
  1.5 0.0 copy-start
  1.5 0.0 copy-start.1
  1.5 35.2 %shard_map.77 = bf16[4,4,64,2048]{3,2,1,0:T(8,128)(2,1)S(1)} custom-call(bf16[16,2048]{1,0:T(8,128)(2,1)S(1)} %copy-done.3), custom_call_target="tpu_custom_call" | custom-call | tf_op jit(solution)/shard_map/pallas_call | solution.py:342
  36.7 0.0 copy-done
  36.7 0.0 copy-done.1
  36.8 0.0 copy-done.4
  36.8 0.0 slice-start
  36.8 7.7 %shard_map.78 = (bf16[896,1024]{1,0:T(8,128)(2,1)S(1)}, f32[8,1024]{1,0:T(8,128)S(1)}) custom-call(bf16[1024,2048]{1,0:T(8,128)(2,1)S(1)} %bitcast.30, f32[2,8192]{1,0:T(2,128)S(1)} %copy-done.4, bf16[2,224,2048]{2,1,0:T(8,128)(2,1)S(1)} %bitcast.31, bf16[2,224,2048]{2,1,0:T(8,128)(2,1)S(1)} %bitcast.32), custom_call_target="tpu_custom_call" | custom-call | tf_op jit(solution)/shard_map/pallas_call | solution.py:368
  44.5 0.0 slice-start.1
  44.5 50.9 %shard_map.79 = bf16[2,4,4,224,256]{4,3,2,1,0:T(8,128)(2,1)S(1)} custom-call(bf16[896,1024]{1,0:T(8,128)(2,1)S(1)} %get-tuple-element.6.part, f32[8,1024]{1,0:T(8,128)S(1)} %get-tuple-element.7.squares), custom_call_target="tpu_custom_call" | custom-call | tf_op jit(solution)/shard_map/pallas_call | solution.py:533
  95.5 0.2 fusion.12
  95.7 0.0 slice-done
  95.7 0.0 slice-done.1
  95.7 1.1 fusion.6
  96.9 1.1 fusion.9
  98.0 0.0 copy-start.2
  98.0 0.1 maximum_bitcast_fusion.part
  98.1 38.1 %shard_map.80 = bf16[2,16,64,512]{3,2,1,0:T(8,128)(2,1)S(1)} custom-call(bf16[4,2,64,512]{3,2,1,0:T(8,128)(2,1)S(1)} %maximum_bitcast_fusion.part), custom_call_target="tpu_custom_call" | custom-call | tf_op jit(solution)/shard_map/pallas_call | solution.py:604
  136.2 0.0 copy-done.2
  136.2 0.7 shard_map.81
  136.9 44.9 %shard_map.82 = f32[8,2,4,2,8,1792]{5,4,3,2,1,0:T(8,128)S(1)} custom-call(f32[4,2,8,1792]{3,2,1,0:T(8,128)S(1)} %bitcast.33), custom_call_target="tpu_custom_call" | custom-call | tf_op jit(solution)/shard_map/pallas_call | solution.py:673
  181.8 71.4 %shard_map.83 = (f32[32,512]{1,0:T(8,128)}, f32[32,512]{1,0:T(8,128)}) custom-call(f32[1024,1792]{1,0:T(8,128)S(1)} %bitcast.27, bf16[2,1024,512]{2,1,0:T(8,128)(2,1)S(1)} %bitcast.29), custom_call_target="tpu_custom_call" | custom-call | tf_op jit(solution)/shard_map/pallas_call | solution.py:186
  (2 shorter events, 0.0 us)
Async XLA Ops:
  0.6 0.8 copy-start.3
  1.5 35.3 %copy-start = (bf16[2,2048,224]{1,2,0:T(8,128)(2,1)S(1)}, bf16[2,2048,224]{1,2,0:T(8,128)(2,1)}, u32[]{:S(2)}) copy-start(bf16[2,2048,224]{1,2,0:T(8,128)(2,1)} %param.8) | copy-start | bytes 5505028
  1.5 35.3 %copy-start.1 = (bf16[2,2048,224]{1,2,0:T(8,128)(2,1)S(1)}, bf16[2,2048,224]{1,2,0:T(8,128)(2,1)}, u32[]{:S(2)}) copy-start(bf16[2,2048,224]{1,2,0:T(8,128)(2,1)} %param.9) | copy-start | bytes 5505028
  1.5 35.3 %copy-start.4 = (f32[2,8192]{1,0:T(2,128)S(1)}, f32[2,8192]{1,0:T(2,128)}, u32[]{:S(2)}) copy-start(f32[2,8192]{1,0:T(2,128)} %gain_ref.1) | copy-start | bytes 196612
  36.8 58.9 %slice-start = ((s8[7340032]{0:T(1024)(128)(4,1)}), s8[3145728]{0:T(1024)(128)(4,1)S(1)}, s32[]{:S(2)}) async-start(s8[7340032]{0:T(1024)(128)(4,1)} %bitcast.38), calls=%async_computation | async-start | bytes 6291456
  44.5 51.2 %slice-start.1 = ((s8[7340032]{0:T(1024)(128)(4,1)}), s8[4194304]{0:T(1024)(128)(4,1)S(1)}, s32[]{:S(2)}) async-start(s8[7340032]{0:T(1024)(128)(4,1)} %bitcast.38), calls=%async_computation.1 | async-start | bytes 8388608
  98.0 38.2 %copy-start.2 = (bf16[512,512]{1,0:T(8,128)(2,1)S(1)}, bf16[512,512]{1,0:T(8,128)(2,1)}, u32[]{:S(2)}) copy-start(bf16[512,512]{1,0:T(8,128)(2,1)} %sketch.1) | copy-start | bytes 1572868

commit v8 on v7

--- a/solution.py
+++ b/solution.py
@@ -455,67 +455,23 @@
                 rows = pl.ds(pl.multiple_of(i * step, step), step)
                 out[c, x, y, rows, lanes] = value.astype(jnp.bfloat16)
 
-    upper, lower = pl.ds(0, units // 2), pl.ds(units // 2, units // 2)
-    every = slice(None)
-    two, rest = pl.ds(0, 2), pl.ds(2, 2)
-
-    def start(h, phase):
+    part_rows = slice(None), pl.ds(0, units // 2), pl.ds(units // 2, units // 2)
+    pending = []
+    for h in range(2):
+        activate(h)
         lanes = pl.ds(h * chunk, chunk)
-        if phase == 0:
-            return (
-                ring(
-                    send,
-                    lambda i: out.at[0, i, y, :, lanes],
-                    lambda i: out.at[0, i, y, upper, lanes],
-                    lambda i: out.at[0, i, y, lower, lanes],
-                    x,
-                    along_x(y),
-                ),
-                ring(
-                    send,
-                    lambda i: out.at[1, x, i, :, lanes],
-                    lambda i: out.at[1, x, i, upper, lanes],
-                    lambda i: out.at[1, x, i, lower, lanes],
-                    y,
-                    along_y(x),
-                ),
-            )
-        return (
-            ring(
-                send,
-                lambda i: out.at[0, every, i, :, lanes],
-                lambda i: out.at[0, two, i, :, lanes],
-                lambda i: out.at[0, rest, i, :, lanes],
-                y,
-                along_y(x),
-            ),
-            ring(
-                send,
-                lambda i: out.at[1, i, every, :, lanes],
-                lambda i: out.at[1, i, two, :, lanes],
-                lambda i: out.at[1, i, rest, :, lanes],
-                x,
-                along_x(y),
-            ),
-        )
-
-    def forward(pair_of_rings):
-        return [copy for one in pair_of_rings for copy in one()]
-
-    def settle(copies):
-        for copy in copies:
-            copy.wait_recv()
-
-    activate(0)
-    rings = start(0, 0)
-    settle(forward(rings))
-    early = start(0, 1)
-    activate(1)
-    rings = start(1, 0)
-    tail = forward(early)
-    settle(forward(rings))
-    tail += forward(start(1, 1))
-    settle(tail)
+
+        def base(i, j, p, lanes=lanes):
+            return out.at[0, i, j, part_rows[p], lanes]
+
+        def instruct(i, j, p, lanes=lanes):
+            return out.at[1, j, i, part_rows[p], lanes]
+
+        plan_a = (base, x, along_x(y), y, along_y(x))
+        plan_b = (instruct, y, along_y(x), x, along_x(y))
+        pending += crossed_rings(send, (plan_a, plan_b))
+    for copy in pending:
+        copy.wait_recv()
     send.finish()
 
 
@@ -530,7 +486,7 @@
         pltpu.VMEM((2, rows, tokens // 2), jnp.bfloat16),
         pltpu.VMEM((8, tokens), jnp.float32),
     ]
-    return remote_call(hidden_kernel, out, 41, 1, 24, scratch)(part, squares)
+    return remote_call(hidden_kernel, out, 89, 1, 24, scratch)(part, squares)
 
 
 def acts_kernel(part, out, landed, send_sem, recv_sem):

time: 253 us -> 251 us (level)
    pallas_call x1, Pallas kernels: 50.9 us -> 46 us  [sum_and_gather_hidden(): return remote_call(hidden_kernel, out, 89, 1, 24, scratch)(part, squares)]
    pallas_call x1, Pallas kernels: 38.1 us -> 40.8 us  [sum_and_gather_acts(): return remote_call(acts_kernel, out, 38, 2, 12, scratch)(part)]
where the time goes in v8:
time: 251 us
  Pallas kernels  247 us (98%)
    pallas_call x1, Pallas kernels, sketch_call(): pl.pallas_call(sketch_kernel, out_shape=(shape, shape), in_specs=[pl.Bloc...  71.4 us
    pallas_call x1, Pallas kernels, sum_and_gather_hidden(): return remote_call(hidden_kernel, out, 89, 1, 24, scratch)(part, squares)  46 us
    pallas_call x1, Pallas kernels, sum_and_gather_rows(): remote_call(rows_kernel, out, 70, 3, 24, scratch)  44.9 us
    pallas_call x1, Pallas kernels, sum_and_gather_acts(): return remote_call(acts_kernel, out, 38, 2, 12, scratch)(part)  40.8 us
    pallas_call x1, Pallas kernels, gather_tokens(): return remote_call(tokens_kernel, out, 43, 0, 12)(tokens)  35.2 us
    pallas_call x1, Pallas kernels, project(): pl.pallas_call(project_kernel, grid=(count // step,), out_shape=(jax.Shap...  7.72 us

profile of v8, /device:TPU:1, one launch (start us, length us, event | category | flops | bytes accessed | tf_op | source)
XLA Modules:
  0.0 251.0 jit_solution(1819879775143972913)
XLA Ops:
  0.6 0.0 copy-start.3
  0.6 0.8 copy-done.3
  1.5 0.0 copy-start
  1.5 0.0 copy-start.1
  1.5 35.2 %shard_map.77 = bf16[4,4,64,2048]{3,2,1,0:T(8,128)(2,1)S(1)} custom-call(bf16[16,2048]{1,0:T(8,128)(2,1)S(1)} %copy-done.3), custom_call_target="tpu_custom_call" | custom-call | tf_op jit(solution)/shard_map/pallas_call | solution.py:342
  36.7 0.0 copy-done
  36.7 0.0 copy-done.1
  36.8 0.0 copy-done.4
  36.8 0.0 slice-start
  36.8 7.7 %shard_map.78 = (bf16[896,1024]{1,0:T(8,128)(2,1)S(1)}, f32[8,1024]{1,0:T(8,128)S(1)}) custom-call(bf16[1024,2048]{1,0:T(8,128)(2,1)S(1)} %bitcast.30, f32[2,8192]{1,0:T(2,128)S(1)} %copy-done.4, bf16[2,224,2048]{2,1,0:T(8,128)(2,1)S(1)} %bitcast.31, bf16[2,224,2048]{2,1,0:T(8,128)(2,1)S(1)} %bitcast.32), custom_call_target="tpu_custom_call" | custom-call | tf_op jit(solution)/shard_map/pallas_call | solution.py:368
  44.5 0.0 slice-start.1
  44.5 46.0 %shard_map.79 = bf16[2,4,4,224,256]{4,3,2,1,0:T(8,128)(2,1)S(1)} custom-call(bf16[896,1024]{1,0:T(8,128)(2,1)S(1)} %get-tuple-element.6.part, f32[8,1024]{1,0:T(8,128)S(1)} %get-tuple-element.7.squares), custom_call_target="tpu_custom_call" | custom-call | tf_op jit(solution)/shard_map/pallas_call | solution.py:489
  90.6 0.2 fusion.12
  90.8 0.0 slice-done
  90.8 0.0 slice-done.1
  90.8 1.1 fusion.6
  92.0 1.1 fusion.9
  93.1 0.0 copy-start.2
  93.1 0.1 maximum_bitcast_fusion.part
  93.2 40.8 %shard_map.80 = bf16[2,16,64,512]{3,2,1,0:T(8,128)(2,1)S(1)} custom-call(bf16[4,2,64,512]{3,2,1,0:T(8,128)(2,1)S(1)} %maximum_bitcast_fusion.part), custom_call_target="tpu_custom_call" | custom-call | tf_op jit(solution)/shard_map/pallas_call | solution.py:560
  134.0 0.0 copy-done.2
  134.0 0.7 shard_map.81
  134.7 44.9 %shard_map.82 = f32[8,2,4,2,8,1792]{5,4,3,2,1,0:T(8,128)S(1)} custom-call(f32[4,2,8,1792]{3,2,1,0:T(8,128)S(1)} %bitcast.33), custom_call_target="tpu_custom_call" | custom-call | tf_op jit(solution)/shard_map/pallas_call | solution.py:629
  179.6 71.4 %shard_map.83 = (f32[32,512]{1,0:T(8,128)}, f32[32,512]{1,0:T(8,128)}) custom-call(f32[1024,1792]{1,0:T(8,128)S(1)} %bitcast.27, bf16[2,1024,512]{2,1,0:T(8,128)(2,1)S(1)} %bitcast.29), custom_call_target="tpu_custom_call" | custom-call | tf_op jit(solution)/shard_map/pallas_call | solution.py:186
  (2 shorter events, 0.0 us)
Async XLA Ops:
  0.6 0.8 copy-start.3
  1.5 35.3 %copy-start = (bf16[2,2048,224]{1,2,0:T(8,128)(2,1)S(1)}, bf16[2,2048,224]{1,2,0:T(8,128)(2,1)}, u32[]{:S(2)}) copy-start(bf16[2,2048,224]{1,2,0:T(8,128)(2,1)} %param.8) | copy-start | bytes 5505028
  1.5 35.3 %copy-start.1 = (bf16[2,2048,224]{1,2,0:T(8,128)(2,1)S(1)}, bf16[2,2048,224]{1,2,0:T(8,128)(2,1)}, u32[]{:S(2)}) copy-start(bf16[2,2048,224]{1,2,0:T(8,128)(2,1)} %param.9) | copy-start | bytes 5505028
  1.5 35.3 %copy-start.4 = (f32[2,8192]{1,0:T(2,128)S(1)}, f32[2,8192]{1,0:T(2,128)}, u32[]{:S(2)}) copy-start(f32[2,8192]{1,0:T(2,128)} %gain_ref.1) | copy-start | bytes 196612
  36.8 54.1 %slice-start = ((s8[7340032]{0:T(1024)(128)(4,1)}), s8[3145728]{0:T(1024)(128)(4,1)S(1)}, s32[]{:S(2)}) async-start(s8[7340032]{0:T(1024)(128)(4,1)} %bitcast.38), calls=%async_computation | async-start | bytes 6291456
  44.5 46.3 %slice-start.1 = ((s8[7340032]{0:T(1024)(128)(4,1)}), s8[4194304]{0:T(1024)(128)(4,1)S(1)}, s32[]{:S(2)}) async-start(s8[7340032]{0:T(1024)(128)(4,1)} %bitcast.38), calls=%async_computation.1 | async-start | bytes 8388608
  93.1 40.9 %copy-start.2 = (bf16[512,512]{1,0:T(8,128)(2,1)S(1)}, bf16[512,512]{1,0:T(8,128)(2,1)}, u32[]{:S(2)}) copy-start(bf16[512,512]{1,0:T(8,128)(2,1)} %sketch.1) | copy-start | bytes 1572868

commit v9 on v8

--- a/solution.py
+++ b/solution.py
@@ -516,8 +516,9 @@
         return out.at[c, chip * 2 + core]
 
     shared = []
-    waiting = []
-    for c in range(2):
+    waiting = [None, None]
+
+    def begin(c):
         for copy in sums[c]:
             copy.wait_recv()
         total = part[m, c].astype(jnp.float32)
@@ -525,24 +526,32 @@
             total += landed[k, c].astype(jnp.float32)
         out[c, z * 2 + core] = total.astype(jnp.bfloat16)
         here = block(c, z)
-        waiting.append((send(here, here, right), send(here, here, left)))
+        waiting[c] = (send(here, here, right), send(here, here, left))
         shared.append(send(here, here, sibling))
+
+    def advance(c, k):
+        before, after = (z + 8 - k) % 8, (z + k) % 8
+        from_left, from_right = waiting[c]
+        near, next_near = block(c, before), block(c, after)
+        on, back = near, next_near
+        if k == 3:
+            on = out.at[c, before * 2 + core, halves[0]]
+            back = out.at[c, after * 2 + core, halves[1]]
+        from_left.wait_recv()
+        next_left = send(on, on, right)
+        from_right.wait_recv()
+        next_right = send(back, back, left)
+        shared.append(send(near, near, sibling))
+        shared.append(send(next_near, next_near, sibling))
+        waiting[c] = (next_left, next_right)
+
+    begin(0)
+    advance(0, 1)
+    begin(1)
     for k in range(1, 4):
-        before, after = (z + 8 - k) % 8, (z + k) % 8
-        for c in range(2):
-            from_left, from_right = waiting[c]
-            near, next_near = block(c, before), block(c, after)
-            on, back = near, next_near
-            if k == 3:
-                on = out.at[c, before * 2 + core, halves[0]]
-                back = out.at[c, after * 2 + core, halves[1]]
-            from_left.wait_recv()
-            next_left = send(on, on, right)
-            from_right.wait_recv()
-            next_right = send(back, back, left)
-            shared.append(send(near, near, sibling))
-            shared.append(send(next_near, next_near, sibling))
-            waiting[c] = (next_left, next_right)
+        if k < 3:
+            advance(0, k + 1)
+        advance(1, k)
     far = (z + 4) % 8
     for c in range(2):
         for copy in waiting[c]:

time: 251 us -> 254 us (1.012)
    pallas_call x1, Pallas kernels: 40.8 us -> 43.6 us  [sum_and_gather_acts(): return remote_call(acts_kernel, out, 38, 2, 12, scratch)(part)]
where the time goes in v9:
time: 254 us
  Pallas kernels  249 us (98%)
    pallas_call x1, Pallas kernels, sketch_call(): pl.pallas_call(sketch_kernel, out_shape=(shape, shape), in_specs=[pl.Bloc...  71.4 us
    pallas_call x1, Pallas kernels, sum_and_gather_hidden(): return remote_call(hidden_kernel, out, 89, 1, 24, scratch)(part, squares)  46 us
    pallas_call x1, Pallas kernels, sum_and_gather_rows(): remote_call(rows_kernel, out, 70, 3, 24, scratch)  44.8 us
    pallas_call x1, Pallas kernels, sum_and_gather_acts(): return remote_call(acts_kernel, out, 38, 2, 12, scratch)(part)  43.6 us
    pallas_call x1, Pallas kernels, gather_tokens(): return remote_call(tokens_kernel, out, 43, 0, 12)(tokens)  35.2 us
    pallas_call x1, Pallas kernels, project(): pl.pallas_call(project_kernel, grid=(count // step,), out_shape=(jax.Shap...  7.72 us

profile of v9, /device:TPU:1, one launch (start us, length us, event | category | flops | bytes accessed | tf_op | source)
XLA Modules:
  0.0 253.6 jit_solution(18261064606289579120)
XLA Ops:
  0.6 0.0 copy-start.3
  0.6 0.8 copy-done.3
  1.5 0.0 copy-start
  1.5 0.0 copy-start.1
  1.5 35.2 %shard_map.77 = bf16[4,4,64,2048]{3,2,1,0:T(8,128)(2,1)S(1)} custom-call(bf16[16,2048]{1,0:T(8,128)(2,1)S(1)} %copy-done.3), custom_call_target="tpu_custom_call" | custom-call | tf_op jit(solution)/shard_map/pallas_call | solution.py:342
  36.7 0.0 copy-done
  36.7 0.0 copy-done.1
  36.8 0.0 copy-done.4
  36.8 0.0 slice-start
  36.8 7.7 %shard_map.78 = (bf16[896,1024]{1,0:T(8,128)(2,1)S(1)}, f32[8,1024]{1,0:T(8,128)S(1)}) custom-call(bf16[1024,2048]{1,0:T(8,128)(2,1)S(1)} %bitcast.30, f32[2,8192]{1,0:T(2,128)S(1)} %copy-done.4, bf16[2,224,2048]{2,1,0:T(8,128)(2,1)S(1)} %bitcast.31, bf16[2,224,2048]{2,1,0:T(8,128)(2,1)S(1)} %bitcast.32), custom_call_target="tpu_custom_call" | custom-call | tf_op jit(solution)/shard_map/pallas_call | solution.py:368
  44.5 0.0 slice-start.1
  44.5 46.0 %shard_map.79 = bf16[2,4,4,224,256]{4,3,2,1,0:T(8,128)(2,1)S(1)} custom-call(bf16[896,1024]{1,0:T(8,128)(2,1)S(1)} %get-tuple-element.6.part, f32[8,1024]{1,0:T(8,128)S(1)} %get-tuple-element.7.squares), custom_call_target="tpu_custom_call" | custom-call | tf_op jit(solution)/shard_map/pallas_call | solution.py:489
  90.6 0.2 fusion.12
  90.8 0.0 slice-done
  90.8 0.0 slice-done.1
  90.8 1.1 fusion.6
  92.0 1.1 fusion.9
  93.1 0.0 copy-start.2
  93.1 0.1 maximum_bitcast_fusion.part
  93.2 43.6 %shard_map.80 = bf16[2,16,64,512]{3,2,1,0:T(8,128)(2,1)S(1)} custom-call(bf16[4,2,64,512]{3,2,1,0:T(8,128)(2,1)S(1)} %maximum_bitcast_fusion.part), custom_call_target="tpu_custom_call" | custom-call | tf_op jit(solution)/shard_map/pallas_call | solution.py:569
  136.7 0.0 copy-done.2
  136.8 0.7 shard_map.81
  137.4 44.8 %shard_map.82 = f32[8,2,4,2,8,1792]{5,4,3,2,1,0:T(8,128)S(1)} custom-call(f32[4,2,8,1792]{3,2,1,0:T(8,128)S(1)} %bitcast.33), custom_call_target="tpu_custom_call" | custom-call | tf_op jit(solution)/shard_map/pallas_call | solution.py:638
  182.3 71.4 %shard_map.83 = (f32[32,512]{1,0:T(8,128)}, f32[32,512]{1,0:T(8,128)}) custom-call(f32[1024,1792]{1,0:T(8,128)S(1)} %bitcast.27, bf16[2,1024,512]{2,1,0:T(8,128)(2,1)S(1)} %bitcast.29), custom_call_target="tpu_custom_call" | custom-call | tf_op jit(solution)/shard_map/pallas_call | solution.py:186
  (2 shorter events, 0.0 us)
Async XLA Ops:
  0.6 0.8 copy-start.3
  1.5 35.3 %copy-start = (bf16[2,2048,224]{1,2,0:T(8,128)(2,1)S(1)}, bf16[2,2048,224]{1,2,0:T(8,128)(2,1)}, u32[]{:S(2)}) copy-start(bf16[2,2048,224]{1,2,0:T(8,128)(2,1)} %param.8) | copy-start | bytes 5505028
  1.5 35.3 %copy-start.1 = (bf16[2,2048,224]{1,2,0:T(8,128)(2,1)S(1)}, bf16[2,2048,224]{1,2,0:T(8,128)(2,1)}, u32[]{:S(2)}) copy-start(bf16[2,2048,224]{1,2,0:T(8,128)(2,1)} %param.9) | copy-start | bytes 5505028
  1.5 35.3 %copy-start.4 = (f32[2,8192]{1,0:T(2,128)S(1)}, f32[2,8192]{1,0:T(2,128)}, u32[]{:S(2)}) copy-start(f32[2,8192]{1,0:T(2,128)} %gain_ref.1) | copy-start | bytes 196612
  36.8 54.1 %slice-start = ((s8[7340032]{0:T(1024)(128)(4,1)}), s8[3145728]{0:T(1024)(128)(4,1)S(1)}, s32[]{:S(2)}) async-start(s8[7340032]{0:T(1024)(128)(4,1)} %bitcast.38), calls=%async_computation | async-start | bytes 6291456
  44.5 46.3 %slice-start.1 = ((s8[7340032]{0:T(1024)(128)(4,1)}), s8[4194304]{0:T(1024)(128)(4,1)S(1)}, s32[]{:S(2)}) async-start(s8[7340032]{0:T(1024)(128)(4,1)} %bitcast.38), calls=%async_computation.1 | async-start | bytes 8388608
  93.1 43.6 %copy-start.2 = (bf16[512,512]{1,0:T(8,128)(2,1)S(1)}, bf16[512,512]{1,0:T(8,128)(2,1)}, u32[]{:S(2)}) copy-start(bf16[512,512]{1,0:T(8,128)(2,1)} %sketch.1) | copy-start | bytes 1572868

commit v10 on v8

--- a/solution.py
+++ b/solution.py
@@ -576,7 +576,7 @@
     def at(chip):
         return {"mp": chip % 4, "dp": (chip // 4) * 2 + core}
 
-    chips = [at((z + k) % 8) for k in range(1, 8)]
+    chips = [at((z + k) % 8) for k in (4, 3, 5, 2, 6, 1, 7)]
     sibling = {"dp": zh * 2 + 1 - core}
     greet(peers + chips + [sibling])
     send = Sender(send_sem, recv_sem)

time: 251 us -> 251 us (level)
  no operation moved by 1% of the time
where the time goes in v10:
time: 251 us
  Pallas kernels  247 us (98%)
    pallas_call x1, Pallas kernels, sketch_call(): pl.pallas_call(sketch_kernel, out_shape=(shape, shape), in_specs=[pl.Bloc...  71.4 us
    pallas_call x1, Pallas kernels, sum_and_gather_hidden(): return remote_call(hidden_kernel, out, 89, 1, 24, scratch)(part, squares)  46 us
    pallas_call x1, Pallas kernels, sum_and_gather_rows(): remote_call(rows_kernel, out, 70, 3, 24, scratch)  44.9 us
    pallas_call x1, Pallas kernels, sum_and_gather_acts(): return remote_call(acts_kernel, out, 38, 2, 12, scratch)(part)  40.8 us
    pallas_call x1, Pallas kernels, gather_tokens(): return remote_call(tokens_kernel, out, 43, 0, 12)(tokens)  35.2 us
    pallas_call x1, Pallas kernels, project(): pl.pallas_call(project_kernel, grid=(count // step,), out_shape=(jax.Shap...  7.72 us

profile of v10, /device:TPU:1, one launch (start us, length us, event | category | flops | bytes accessed | tf_op | source)
XLA Modules:
  0.0 250.9 jit_solution(17735222820910404892)
XLA Ops:
  0.6 0.0 copy-start.3
  0.6 0.8 copy-done.3
  1.5 0.0 copy-start
  1.5 0.0 copy-start.4
  1.5 35.2 %shard_map.77 = bf16[4,4,64,2048]{3,2,1,0:T(8,128)(2,1)S(1)} custom-call(bf16[16,2048]{1,0:T(8,128)(2,1)S(1)} %copy-done.3), custom_call_target="tpu_custom_call" | custom-call | tf_op jit(solution)/shard_map/pallas_call | solution.py:342
  36.7 0.0 copy-done
  36.7 0.0 copy-done.1
  36.8 0.0 copy-done.4
  36.8 0.0 slice-start
  36.8 7.7 %shard_map.78 = (bf16[896,1024]{1,0:T(8,128)(2,1)S(1)}, f32[8,1024]{1,0:T(8,128)S(1)}) custom-call(bf16[1024,2048]{1,0:T(8,128)(2,1)S(1)} %bitcast.30, f32[2,8192]{1,0:T(2,128)S(1)} %copy-done.4, bf16[2,224,2048]{2,1,0:T(8,128)(2,1)S(1)} %bitcast.31, bf16[2,224,2048]{2,1,0:T(8,128)(2,1)S(1)} %bitcast.32), custom_call_target="tpu_custom_call" | custom-call | tf_op jit(solution)/shard_map/pallas_call | solution.py:368
  44.5 0.0 slice-start.1
  44.5 46.0 %shard_map.79 = bf16[2,4,4,224,256]{4,3,2,1,0:T(8,128)(2,1)S(1)} custom-call(bf16[896,1024]{1,0:T(8,128)(2,1)S(1)} %get-tuple-element.6.part, f32[8,1024]{1,0:T(8,128)S(1)} %get-tuple-element.7.squares), custom_call_target="tpu_custom_call" | custom-call | tf_op jit(solution)/shard_map/pallas_call | solution.py:489
  90.6 0.2 fusion.12
  90.8 0.0 slice-done
  90.8 0.0 slice-done.1
  90.8 1.1 fusion.6
  92.0 1.1 fusion.9
  93.1 0.0 copy-start.2
  93.1 0.1 maximum_bitcast_fusion.part
  93.2 40.8 %shard_map.80 = bf16[2,16,64,512]{3,2,1,0:T(8,128)(2,1)S(1)} custom-call(bf16[4,2,64,512]{3,2,1,0:T(8,128)(2,1)S(1)} %maximum_bitcast_fusion.part), custom_call_target="tpu_custom_call" | custom-call | tf_op jit(solution)/shard_map/pallas_call | solution.py:560
  134.0 0.0 copy-done.2
  134.0 0.7 shard_map.81
  134.7 44.9 %shard_map.82 = f32[8,2,4,2,8,1792]{5,4,3,2,1,0:T(8,128)S(1)} custom-call(f32[4,2,8,1792]{3,2,1,0:T(8,128)S(1)} %bitcast.33), custom_call_target="tpu_custom_call" | custom-call | tf_op jit(solution)/shard_map/pallas_call | solution.py:629
  179.6 71.4 %shard_map.83 = (f32[32,512]{1,0:T(8,128)}, f32[32,512]{1,0:T(8,128)}) custom-call(f32[1024,1792]{1,0:T(8,128)S(1)} %bitcast.27, bf16[2,1024,512]{2,1,0:T(8,128)(2,1)S(1)} %bitcast.29), custom_call_target="tpu_custom_call" | custom-call | tf_op jit(solution)/shard_map/pallas_call | solution.py:186
  (2 shorter events, 0.0 us)
Async XLA Ops:
  0.6 0.8 copy-start.3
  1.5 35.3 %copy-start = (bf16[2,2048,224]{1,2,0:T(8,128)(2,1)S(1)}, bf16[2,2048,224]{1,2,0:T(8,128)(2,1)}, u32[]{:S(2)}) copy-start(bf16[2,2048,224]{1,2,0:T(8,128)(2,1)} %param.8) | copy-start | bytes 5505028
  1.5 35.3 %copy-start.1 = (bf16[2,2048,224]{1,2,0:T(8,128)(2,1)S(1)}, bf16[2,2048,224]{1,2,0:T(8,128)(2,1)}, u32[]{:S(2)}) copy-start(bf16[2,2048,224]{1,2,0:T(8,128)(2,1)} %param.9) | copy-start | bytes 5505028
  1.5 35.3 %copy-start.4 = (f32[2,8192]{1,0:T(2,128)S(1)}, f32[2,8192]{1,0:T(2,128)}, u32[]{:S(2)}) copy-start(f32[2,8192]{1,0:T(2,128)} %gain_ref.1) | copy-start | bytes 196612
  36.8 54.1 %slice-start = ((s8[7340032]{0:T(1024)(128)(4,1)}), s8[3145728]{0:T(1024)(128)(4,1)S(1)}, s32[]{:S(2)}) async-start(s8[7340032]{0:T(1024)(128)(4,1)} %bitcast.38), calls=%async_computation | async-start | bytes 6291456
  44.5 46.3 %slice-start.1 = ((s8[7340032]{0:T(1024)(128)(4,1)}), s8[4194304]{0:T(1024)(128)(4,1)S(1)}, s32[]{:S(2)}) async-start(s8[7340032]{0:T(1024)(128)(4,1)} %bitcast.38), calls=%async_computation.1 | async-start | bytes 8388608
  93.1 40.9 %copy-start.2 = (bf16[512,512]{1,0:T(8,128)(2,1)S(1)}, bf16[512,512]{1,0:T(8,128)(2,1)}, u32[]{:S(2)}) copy-start(bf16[512,512]{1,0:T(8,128)(2,1)} %sketch.1) | copy-start | bytes 1572868
